TPU v7x, 32 devices: a whole 2x2x4 slice. The times are simulated.
32 devices in a mesh: shard: 4 (over y, core), rep: 8 (over z, x).
Axes of the slice: x: 2, y: 2, z: 4, core: 2. Of those that a mesh axis runs over, the one named last changes fastest.
Arguments:
- layer_input: bfloat16 [256, 197, 768], P(('shard', 'rep')), may hold values from -6 to 6
- out_cotangent: bfloat16 [256, 197, 768], P(('shard', 'rep')), may hold values from -6 to 6
- attention_params: float32 [2363136], P('shard'), may hold values from -2 to 2.5
- attention_moments: float32 [2, 2363136], P(None, 'shard'), may hold values from -0.2 to 0.2, as said below
- feedforward_params: float32 [4723968], P('shard'), may hold values from -2 to 2.5
- feedforward_moments: float32 [2, 4723968], P(None, 'shard'), may hold values from -0.2 to 0.2, as said below
- step_count: int32 [1], replicated, may hold values from 1 to 20
Outputs:
- layer_output: bfloat16 [256, 197, 768], P(('shard', 'rep'))
- input_grad: bfloat16 [256, 197, 768], P(('shard', 'rep'))
- attention_grad: float32 [2363136], P('shard')
- feedforward_grad: float32 [4723968], P('shard')
- attention_change: float32 [2363136], P('shard')
- attention_moments_new: float32 [2, 2363136], P(None, 'shard')
- feedforward_change: float32 [4723968], P('shard')
- feedforward_moments_new: float32 [2, 4723968], P(None, 'shard')
Inputs may be any that keep to these rules, and one draw needn't show every extreme that they name: `attention_moments`: row 1, the second moments, is positive. `feedforward_moments`: row 1, the second moments, is positive.
All inputs are finite; a program needn't handle non-finite values.
Results may differ from a plain program's by a relative error of at most 0.017.
The roundings to bfloat16 on the way count: a program that leaves them out, or rounds other values in their place, can miss the bound.
Values may be sent and summed in bfloat16 or wider, within the bound.
No kernel may reach another device: no remote copies, remote signals or barrier semaphores. Data moves between devices by JAX's collectives and lax.ppermute only.
A program may use at most 384 MiB of HBM per device.

v0:
```python
import jax
import jax.numpy as jnp
from jax import lax
from jax.sharding import PartitionSpec as P

D = 768
HEADS = 12
HEAD_DIM = 64
FF = 3072


ln_eps = 1e-06
beta_one = 0.9
beta_two = 0.999
adam_eps = 1e-08
rate_matrix = 0.01
rate_vector = 0.1
decay_matrix = 0.05
root_half = 0.7071067811865476
inv_root_tau = 0.3989422804014327


def product(form, left, right):
    return jnp.einsum(form, left, right, preferred_element_type=jnp.float32)


def times_transposed(left, right):
    return lax.dot_general(
        left, right, (((1,), (1,)), ((), ())), preferred_element_type=jnp.float32
    )


def transposed_times(left, right):
    return lax.dot_general(
        left, right, (((0,), (0,)), ((), ())), preferred_element_type=jnp.float32
    )


def split_flat(flat_vec, lengths):
    starts = [0]
    for length in lengths:
        starts.append(starts[-1] + length)
    return [
        flat_vec[starts[position] : starts[position] + lengths[position]]
        for position in range(len(lengths))
    ]


def attention_lengths(model_width):
    return [
        model_width,
        model_width,
        3 * model_width * model_width,
        model_width,
        model_width,
        model_width * model_width,
        model_width,
    ]


def feedforward_lengths(model_width, hidden_width):
    return [
        model_width,
        model_width,
        model_width * hidden_width,
        hidden_width,
        hidden_width * model_width,
        model_width,
    ]


def matrix_mask(lengths, matrix_slots, positions):
    starts = [0]
    for length in lengths:
        starts.append(starts[-1] + length)
    is_matrix = jnp.zeros(positions.shape, bool)
    for matrix_slot in matrix_slots:
        inside = (positions >= starts[matrix_slot]) & (
            positions < starts[matrix_slot] + lengths[matrix_slot]
        )
        is_matrix = is_matrix | inside
    return is_matrix


def unpack_weights(attention_flat, feedforward_flat, model_width, hidden_width):
    gain_one, shift_one, qkv_flat, query_bias, value_bias, proj_flat, proj_bias = split_flat(
        attention_flat, attention_lengths(model_width)
    )
    gain_two, shift_two, up_flat, up_bias, down_flat, down_bias = split_flat(
        feedforward_flat, feedforward_lengths(model_width, hidden_width)
    )
    return (
        gain_one,
        shift_one,
        qkv_flat.reshape(model_width, 3 * model_width),
        query_bias,
        value_bias,
        proj_flat.reshape(model_width, model_width),
        proj_bias,
        gain_two,
        shift_two,
        up_flat.reshape(model_width, hidden_width),
        up_bias,
        down_flat.reshape(hidden_width, model_width),
        down_bias,
    )


def norm_forward(values, gain_vec, shift_vec):
    center = values - jnp.mean(values, axis=-1, keepdims=True)
    spread = lax.rsqrt(jnp.mean(center * center, axis=-1, keepdims=True) + ln_eps)
    normed = center * spread
    return (normed * gain_vec.astype(jnp.float32) + shift_vec.astype(jnp.float32), normed, spread)


def norm_backward(grad_out, normed, spread, gain_vec):
    grad_normed = grad_out * gain_vec.astype(jnp.float32)
    return spread * (
        grad_normed
        - jnp.mean(grad_normed, axis=-1, keepdims=True)
        - normed * jnp.mean(grad_normed * normed, axis=-1, keepdims=True)
    )


def gelu_value(values):
    return 0.5 * values * (1.0 + lax.erf(values * root_half))


def gelu_slope(values):
    return (
        0.5 * (1.0 + lax.erf(values * root_half))
        + values * jnp.exp(-0.5 * values * values) * inv_root_tau
    )


def forward_pass(inputs, weights):
    (
        gain_one,
        shift_one,
        qkv_weight,
        query_bias,
        value_bias,
        proj_weight,
        proj_bias,
        gain_two,
        shift_two,
        up_weight,
        up_bias,
        down_weight,
        down_bias,
    ) = weights
    image_count, seq_len, model_width = inputs.shape
    token_rows = inputs.reshape(image_count * seq_len, model_width).astype(jnp.float32)
    normed_out, normed_one, spread_one = norm_forward(token_rows, gain_one, shift_one)
    first_in = normed_out.astype(jnp.bfloat16)
    zero_bias = jnp.zeros(query_bias.shape, jnp.float32)
    qkv_bias = jnp.concatenate(
        [query_bias.astype(jnp.float32), zero_bias, value_bias.astype(jnp.float32)]
    )
    projected = jnp.dot(first_in, qkv_weight, preferred_element_type=jnp.float32) + qkv_bias
    projected = projected.astype(jnp.bfloat16)
    head_shape = (image_count, seq_len, HEADS, HEAD_DIM)
    query_part = projected[:, :model_width].reshape(head_shape)
    key_part = projected[:, model_width : 2 * model_width].reshape(head_shape)
    value_part = projected[:, 2 * model_width :].reshape(head_shape)
    scores = product("bqhd,bkhd->bhqk", query_part, key_part) * HEAD_DIM ** (-0.5)
    row_top = jnp.max(scores, axis=-1, keepdims=True)
    log_total = row_top + jnp.log(jnp.sum(jnp.exp(scores - row_top), axis=-1, keepdims=True))
    attn_probs = jnp.exp(scores - log_total).astype(jnp.bfloat16)
    attended = product("bhqk,bkhd->bqhd", attn_probs, value_part).astype(jnp.bfloat16)
    attended = attended.reshape(image_count * seq_len, model_width)
    hidden_rows = (
        token_rows
        + jnp.dot(attended, proj_weight, preferred_element_type=jnp.float32)
        + proj_bias.astype(jnp.float32)
    )
    second_out, normed_two, spread_two = norm_forward(hidden_rows, gain_two, shift_two)
    second_in = second_out.astype(jnp.bfloat16)
    pre_act = jnp.dot(second_in, up_weight, preferred_element_type=jnp.float32) + up_bias.astype(
        jnp.float32
    )
    act_low = gelu_value(pre_act).astype(jnp.bfloat16)
    result_rows = (
        hidden_rows
        + jnp.dot(act_low, down_weight, preferred_element_type=jnp.float32)
        + down_bias.astype(jnp.float32)
    )
    saved = (
        normed_one,
        spread_one,
        first_in,
        query_part,
        key_part,
        value_part,
        log_total,
        attended,
        normed_two,
        spread_two,
        second_in,
        pre_act,
        act_low,
    )
    return (result_rows, saved)


def feedforward_backward(saved, cot_rows, weights, image_total):
    (
        normed_one,
        spread_one,
        first_in,
        query_part,
        key_part,
        value_part,
        log_total,
        attended,
        normed_two,
        spread_two,
        second_in,
        pre_act,
        act_low,
    ) = saved
    (
        gain_one,
        shift_one,
        qkv_weight,
        query_bias,
        value_bias,
        proj_weight,
        proj_bias,
        gain_two,
        shift_two,
        up_weight,
        up_bias,
        down_weight,
        down_bias,
    ) = weights
    cot_wide = cot_rows.astype(jnp.float32)
    grad_act = times_transposed(cot_rows, down_weight)
    grad_pre = grad_act * gelu_slope(pre_act)
    grad_pre_low = grad_pre.astype(jnp.bfloat16)
    grad_second = times_transposed(grad_pre_low, up_weight)
    grad_hidden = cot_wide + norm_backward(grad_second, normed_two, spread_two, gain_two)
    feed_grads = (
        jnp.concatenate(
            [
                jnp.sum(grad_second * normed_two, axis=0),
                jnp.sum(grad_second, axis=0),
                transposed_times(second_in, grad_pre_low).reshape(-1),
                jnp.sum(grad_pre, axis=0),
                transposed_times(act_low, cot_rows).reshape(-1),
                jnp.sum(cot_wide, axis=0),
            ]
        )
        / image_total
    )
    return (grad_hidden, feed_grads)


def attention_backward(saved, grad_hidden, weights, image_total):
    (
        normed_one,
        spread_one,
        first_in,
        query_part,
        key_part,
        value_part,
        log_total,
        attended,
        normed_two,
        spread_two,
        second_in,
        pre_act,
        act_low,
    ) = saved
    (
        gain_one,
        shift_one,
        qkv_weight,
        query_bias,
        value_bias,
        proj_weight,
        proj_bias,
        gain_two,
        shift_two,
        up_weight,
        up_bias,
        down_weight,
        down_bias,
    ) = weights
    image_count, seq_len = (query_part.shape[0], query_part.shape[1])
    token_count = image_count * seq_len
    model_width = HEADS * HEAD_DIM
    grad_hidden_low = grad_hidden.astype(jnp.bfloat16)
    grad_attended = times_transposed(grad_hidden_low, proj_weight).astype(jnp.bfloat16)
    grad_attended = grad_attended.reshape(image_count, seq_len, HEADS, HEAD_DIM)
    scores = product("bqhd,bkhd->bhqk", query_part, key_part) * HEAD_DIM ** (-0.5)
    probs_wide = jnp.exp(scores - log_total)
    attn_probs = probs_wide.astype(jnp.bfloat16)
    grad_values = product("bhqk,bqhd->bkhd", attn_probs, grad_attended)
    grad_probs = product("bqhd,bkhd->bhqk", grad_attended, value_part)
    row_delta = jnp.sum(probs_wide * grad_probs, axis=-1, keepdims=True)
    grad_scores = (probs_wide * (grad_probs - row_delta) * HEAD_DIM ** (-0.5)).astype(jnp.bfloat16)
    grad_queries = product("bhqk,bkhd->bqhd", grad_scores, key_part).reshape(
        token_count, model_width
    )
    grad_keys = product("bhqk,bqhd->bkhd", grad_scores, query_part).reshape(
        token_count, model_width
    )
    grad_values = grad_values.reshape(token_count, model_width)
    grad_qkv = jnp.concatenate(
        [
            grad_queries.astype(jnp.bfloat16),
            grad_keys.astype(jnp.bfloat16),
            grad_values.astype(jnp.bfloat16),
        ],
        axis=1,
    )
    grad_first = times_transposed(grad_qkv, qkv_weight)
    grad_rows = grad_hidden + norm_backward(grad_first, normed_one, spread_one, gain_one)
    attn_grads = (
        jnp.concatenate(
            [
                jnp.sum(grad_first * normed_one, axis=0),
                jnp.sum(grad_first, axis=0),
                transposed_times(first_in, grad_qkv).reshape(-1),
                jnp.sum(grad_queries, axis=0),
                jnp.sum(grad_values, axis=0),
                transposed_times(attended, grad_hidden_low).reshape(-1),
                jnp.sum(grad_hidden, axis=0),
            ]
        )
        / image_total
    )
    return (grad_rows, attn_grads)


def adam_change(params, moments, grads, step_count, lengths, matrix_slots, offset):
    positions = jnp.arange(params.shape[0], dtype=jnp.int32) + offset
    is_matrix = matrix_mask(lengths, matrix_slots, positions)
    step_wide = step_count[0].astype(jnp.float32)
    first_moment = beta_one * moments[0] + (1.0 - beta_one) * grads
    second_moment = beta_two * moments[1] + (1.0 - beta_two) * grads * grads
    first_hat = first_moment / (1.0 - jnp.power(beta_one, step_wide))
    second_hat = second_moment / (1.0 - jnp.power(beta_two, step_wide))
    step_rate = jnp.where(is_matrix, rate_matrix, rate_vector)
    decay_rate = jnp.where(is_matrix, decay_matrix, 0.0)
    change = step_rate * (first_hat / (jnp.sqrt(second_hat) + adam_eps) + decay_rate * params)
    return (change, jnp.stack([first_moment, second_moment]))


def body(
    layer_input,
    out_cotangent,
    attention_params,
    attention_moments,
    feedforward_params,
    feedforward_moments,
    step_count,
):
    image_total = layer_input.shape[0] * lax.axis_size("shard") * lax.axis_size("rep")
    low_attention = attention_params.astype(jnp.bfloat16)
    low_feed = feedforward_params.astype(jnp.bfloat16)
    full_attention, full_feed = (
        lax.all_gather(low_attention, "shard", axis=0, tiled=True),
        lax.all_gather(low_feed, "shard", axis=0, tiled=True),
    )
    weights_ahead = unpack_weights(full_attention, full_feed, D, FF)
    result_rows, saved = forward_pass(layer_input, weights_ahead)
    layer_output = result_rows.astype(jnp.bfloat16).reshape(layer_input.shape)
    again_attention, again_feed = (
        lax.all_gather(low_attention, "shard", axis=0, tiled=True),
        lax.all_gather(low_feed, "shard", axis=0, tiled=True),
    )
    weights_behind = unpack_weights(again_attention, again_feed, D, FF)
    cot_rows = out_cotangent.reshape(layer_input.shape[0] * layer_input.shape[1], D)
    grad_hidden, feed_grads = feedforward_backward(saved, cot_rows, weights_behind, image_total)
    grad_rows, attn_grads = attention_backward(saved, grad_hidden, weights_behind, image_total)
    attn_share, feed_share = (
        lax.psum_scatter(attn_grads, "shard", scatter_dimension=0, tiled=True),
        lax.psum_scatter(feed_grads, "shard", scatter_dimension=0, tiled=True),
    )
    attn_total, feed_total = lax.psum((attn_share, feed_share), "rep")
    input_grad = grad_rows.astype(jnp.bfloat16).reshape(layer_input.shape)
    attention_offset = lax.axis_index("shard") * attention_params.shape[0]
    feed_offset = lax.axis_index("shard") * feedforward_params.shape[0]
    attention_change, attention_moments_new = adam_change(
        attention_params,
        attention_moments,
        attn_total,
        step_count,
        attention_lengths(D),
        [2, 5],
        attention_offset,
    )
    feedforward_change, feedforward_moments_new = adam_change(
        feedforward_params,
        feedforward_moments,
        feed_total,
        step_count,
        feedforward_lengths(D, FF),
        [2, 4],
        feed_offset,
    )
    return (
        layer_output,
        input_grad,
        attn_total,
        feed_total,
        attention_change,
        attention_moments_new,
        feedforward_change,
        feedforward_moments_new,
    )


def solution(mesh):
    in_specs = (
        P(("shard", "rep"), None, None),
        P(("shard", "rep"), None, None),
        P("shard"),
        P(None, "shard"),
        P("shard"),
        P(None, "shard"),
        P(),
    )
    out_specs = (
        P(("shard", "rep"), None, None),
        P(("shard", "rep"), None, None),
        P("shard"),
        P("shard"),
        P("shard"),
        P(None, "shard"),
        P("shard"),
        P(None, "shard"),
    )
    return jax.shard_map(body, mesh=mesh, in_specs=in_specs, out_specs=out_specs, check_vma=False)
```

profile of v0, /device:TPU:0, one launch (start us, length us, event | category | flops | bytes accessed | tf_op | source)
XLA Modules:
  0.0 1849.7 jit_solution(6545273701394707535)
XLA Ops:
  16.0 19.0 %dynamic-update-slice = bf16[2363136]{0:T(1024)(128)(2,1)} dynamic-update-slice(bf16[2363136]{0:T(1024)(128)(2,1)} %broadcast.130, bf16[590784]{0:T(1024)(128)(2,1)S(1)} %convert_element_type.126, u32[]{:T(128)} %bitcast) | dynamic-update-slice | bytes 2363140
  35.0 4.2 broadcast.131
  39.2 36.3 %dynamic-update-slice.1 = bf16[4723968]{0:T(1024)(128)(2,1)} dynamic-update-slice(bf16[4723968]{0:T(1024)(128)(2,1)} %broadcast.131, bf16[1180992]{0:T(1024)(128)(2,1)S(1)} %convert_element_type.138, u32[]{:T(128)} %bitcast.2) | dynamic-update-slice | bytes 4723972
  82.9 6.5 reshape.221
  99.6 226.2 %all-reduce.15.cloned.1.call-done = (bf16[2363136]{0:T(1024)(128)(2,1)}, bf16[4723968]{0:T(1024)(128)(2,1)}) async-done(((bf16[2363136]{0:T(1024)(128)(2,1)}, bf16[4723968]{0:T(1024)(128)(2,1)}), (bf16[2363136]{0:T(1024)(128)(2,1)}, bf16[4723968]{0:T(1024)(128)(2,1)})) %all-reduce.15.cloned.1.call-update) | async-done | bytes 14174224
  325.8 4.0 slice.110
  334.9 4.7 fusion.72
  342.6 3.9 convert_element_type.130
  346.5 5.2 reshape.207
  351.6 8.4 add_convert_fusion
  362.8 6.4 reshape.234
  369.2 7.3 copy.96
  376.5 8.3 reshape.235
  384.8 8.6 copy.94
  393.4 8.3 reshape.236
  401.6 9.0 copy.95
  410.6 12.4 multiply_reduce_fusion.1
  423.0 11.8 exponential_reduce_fusion
  434.8 10.4 convert_bitcast_fusion.1
  445.2 3.9 copy.98
  449.1 6.3 reshape.211
  458.8 8.2 reshape.212
  467.0 5.9 fusion.75
  475.8 9.2 slice.102
  485.0 18.2 multiply_convert_fusion.1
  503.2 19.6 %fusion.78 = (f32[3072]{0:T(1024)}, bf16[1576,3072]{1,0:T(8,128)(2,1)}) fusion(f32[1576,3072]{1,0:T(8,128)} %get-tuple-element.86, f32[3072]{0:T(1024)S(1)} %copy-done.26, bf16[3072,768]{1,0:T(8,128)(2,1)S(1)} %copy-done.13, bf16[1576,768]{1,0:T(8,128)(2,1)S(1)} %copy-done.6), kind=kOutput, calls=%fused_computation.139 | convolution fusion | flops 7494595584 | bytes 36212736 | tf_op jit(solution)/shard_map/dot_general | solution.py:28
  522.8 16.4 multiply_reduce_fusion.2
  539.2 4.3 fusion.71
  549.3 8.3 reshape.237
  557.6 8.6 copy.101
  566.1 11.3 fusion.79
  577.5 31.5 %bitcast_convert_fusion.1 = (bf16[8,197,12,64]{1,3,2,0:T(8,128)(2,1)}, f32[8,12,64,197]{3,2,1,0:T(8,128)}) fusion(bf16[8,197,12,64]{1,3,2,0:T(8,128)(2,1)} %copy.95, f32[8,12,197,197]{2,3,1,0:T(8,128)} %fusion.79, f32[8,12,197,197]{2,3,1,0:T(8,128)} %get-tuple-element.82, f32[8,12,197]{2,1,0:T(8,128)S(1)} %log_add_fusion), kind=kOutput, calls=%fused_computation.29 | convolution fusion | flops 511645440 | bytes 39563904 | tf_op jit(solution)/shard_map/bhqk,bkhd->bqhd/dot_general | solution.py:24
  609.0 29.2 %convert_bitcast_fusion = bf16[8,197,12,64]{1,3,2,0:T(8,128)(2,1)} fusion(bf16[8,197,12,64]{1,3,2,0:T(8,128)(2,1)} %copy.94, f32[8,12,197,197]{2,3,1,0:T(8,128)} %fusion.79, f32[8,12,197,197]{2,3,1,0:T(8,128)} %get-tuple-element.82, f32[8,12,197]{2,1,0:T(8,128)S(1)} %log_add_fusion), kind=kOutput, calls=%fused_computation.71 | convolution fusion | flops 511645440 | bytes 34722432 | tf_op jit(solution)/shard_map/bhqk,bqhd->bkhd/dot_general | solution.py:24
  638.3 14.0 bitcast_convert_fusion
  652.2 3.9 copy.105
  656.2 4.5 convert_element_type.152
  666.3 4.4 convert_element_type.155
  670.7 5.7 copy.111
  676.4 6.6 convert_element_type.157
  684.7 4.2 constant_dynamic-update-slice_fusion
  689.0 13.4 multiply_reduce_fusion.3
  702.4 13.4 fusion.39
  719.6 14.4 fusion.36
  734.0 7.9 reshape.217
  753.4 60.8 %dynamic-update-slice.10 = f32[2363136]{0:T(1024)} dynamic-update-slice(f32[2363136]{0:T(1024)} %constant_dynamic-update-slice_fusion.5, f32[1769472]{0:T(1024)} %reshape.217, s32[]{} %constant.116) | dynamic-update-slice | bytes 14155780
  818.9 10.1 broadcast_multiply_fusion.1
  829.0 5.9 copy.126
  834.9 13.7 fusion.80
  848.6 10.8 reshape.220
  862.0 80.6 %dynamic-update-slice.4 = f32[4723968]{0:T(1024)} dynamic-update-slice(f32[4723968]{0:T(1024)} %constant_dynamic-update-slice_fusion.6, f32[2359296]{0:T(1024)} %bitcast.67, s32[]{} %constant.116) | dynamic-update-slice | bytes 18874372
  943.9 80.2 %dynamic-update-slice.6 = f32[4723968]{0:T(1024)} dynamic-update-slice(f32[4723968]{0:T(1024)} %constant_dynamic-update-slice_fusion.12, f32[2359296]{0:T(1024)} %reshape.220, s32[]{} %constant.118) | dynamic-update-slice | bytes 18874372
  1025.4 14.5 broadcast_multiply_fusion
  1041.1 474.9 %all-reduce.13.cloned.1.call-done = (f32[2363136]{0:T(1024)}, f32[4723968]{0:T(1024)}) async-done(((f32[2363136]{0:T(1024)}, f32[4723968]{0:T(1024)}), (f32[2363136]{0:T(1024)}, f32[4723968]{0:T(1024)})) %all-reduce.13.cloned.1.call-update) | async-done | bytes 28348432
  1519.8 4.7 dynamic-slice.5
  1524.5 10.5 slice_multiply_fusion.1
  1535.8 55.5 %multiply_reduce_fusion.8 = (f32[1180992]{0:T(1024)}, f32[1180992]{0:T(1024)}) fusion(f32[2,1180992]{1,0:T(2,128)} %param.12), kind=kLoop, calls=%fused_computation.62 | loop fusion | flops 2361984 | bytes 18895872 | tf_op jit(solution)/shard_map/mul | solution.py:342
  1591.3 13.1 add_convert_fusion.3
  1608.7 7.6 add_convert_fusion.2
  1620.6 140.2 %all-reduce.11.cloned.1.call-done = (f32[590784]{0:T(1024)}, f32[1180992]{0:T(1024)}) async-done(((f32[590784]{0:T(1024)}, f32[1180992]{0:T(1024)}), (f32[590784]{0:T(1024)}, f32[1180992]{0:T(1024)})) %all-reduce.11.cloned.1.call-update) | async-done | bytes 7087120 | tf_op jit(solution)/shard_map/psum | solution.py:382
  1760.9 10.0 add_multiply_fusion
  1770.9 22.0 %stack.22 = f32[1,1180992]{1,0:T(1,128)S(1)} reshape(f32[1180992]{0:T(1024)S(1)} %get-tuple-element.57) | data formatting | bytes 9447936 | tf_op jit(solution)/shard_map/stack | solution.py:348
  1793.0 22.1 %stack.21 = f32[1,1180992]{1,0:T(1,128)S(1)} reshape(f32[1180992]{0:T(1024)S(1)} %get-tuple-element.58) | data formatting | bytes 9447936 | tf_op jit(solution)/shard_map/stack | solution.py:348
  1818.4 7.3 pad_maximum_fusion.1
  1825.7 13.3 pad_maximum_fusion
  (172 shorter events, 99.9 us)
Async XLA Ops:
  7.2 318.6 %all-reduce.15.cloned.1.call-start = ((), (), s32[]{:S(2)}) async-start(), calls=%async_computation.2 | async-start | bytes 28352512
  7.2 4.3 copy-start.31
  75.5 1.7 copy-start
  75.6 1440.5 %all-reduce.13.cloned.1.call-start = ((), (), s32[]{:S(2)}) async-start(), calls=%async_computation.1 | async-start | bytes 56705024
  325.8 8.5 copy-start.12
  334.2 5.3 copy-start.18
  334.2 5.3 copy-start.22
  340.7 5.8 copy-start.4
  458.8 8.2 copy-start.28
  472.9 2.2 copy-start.2
  475.7 9.3 copy-start.26
  485.0 18.2 copy-start.6
  485.0 18.2 copy-start.13
  485.0 37.8 %slice-start.2 = ((s8[4841472]{0:T(1024)(128)(4,1)}), s8[4194304]{0:T(1024)(128)(4,1)S(1)}, s32[]{:S(2)}) async-start(s8[4841472]{0:T(1024)(128)(4,1)} %bitcast.70), calls=%async_computation.5 | async-start | bytes 8388608
  503.2 19.6 %slice-start.3 = ((s8[4841472]{0:T(1024)(128)(4,1)}), s8[647168]{0:T(1024)(128)(4,1)S(1)}, s32[]{:S(2)}) async-start(s8[4841472]{0:T(1024)(128)(4,1)} %bitcast.70), calls=%async_computation.6 | async-start | bytes 1294336
  539.2 6.5 copy-start.17
  543.5 2.2 copy-start.3
  609.0 29.3 %copy-start.1 = (bf16[8,197,12,64]{1,3,2,0:T(8,128)(2,1)S(1)}, bf16[8,197,12,64]{1,3,2,0:T(8,128)(2,1)}, u32[]{:S(2)}) copy-start(bf16[8,197,12,64]{1,3,2,0:T(8,128)(2,1)} %copy.101) | copy-start | bytes 7262212
  660.7 3.5 copy-start.15
  670.7 12.3 copy-start.5
  676.4 12.5 slice-start
  683.0 5.9 slice-start.1
  683.0 5.9 copy-start.14
  683.0 5.9 copy-start.19
  683.0 5.9 copy-start.20
  683.1 5.9 copy-start.21
  684.7 31.1 %slice-start.8 = ((s8[4841472]{0:T(1024)(128)(4,1)}), s8[4194304]{0:T(1024)(128)(4,1)S(1)}, s32[]{:S(2)}) async-start(s8[4841472]{0:T(1024)(128)(4,1)} %bitcast.76), calls=%async_computation.11 | async-start | bytes 8388608
  688.9 13.4 copy-start.23
  689.0 26.9 %slice-start.9 = ((s8[4841472]{0:T(1024)(128)(4,1)}), s8[647168]{0:T(1024)(128)(4,1)S(1)}, s32[]{:S(2)}) async-start(s8[4841472]{0:T(1024)(128)(4,1)} %bitcast.76), calls=%async_computation.12 | async-start | bytes 1294336
  689.0 30.6 %slice-start.4 = ((s8[4841472]{0:T(1024)(128)(4,1)}), s8[4194304]{0:T(1024)(128)(4,1)S(1)}, s32[]{:S(2)}) async-start(s8[4841472]{0:T(1024)(128)(4,1)} %bitcast.72), calls=%async_computation.7 | async-start | bytes 8388608
  702.4 13.5 copy-start.16
  702.4 17.2 slice-start.5
  818.3 10.7 slice-start.12
  818.9 10.1 slice-start.13
  818.9 10.1 slice-start.14
  829.0 6.0 copy-start.7
  848.6 10.8 copy-start.30
  848.6 12.1 copy-start.29
  862.0 80.6 %copy-start.25 = (f32[3072]{0:T(1024)S(1)}, f32[3072]{0:T(1024)}, u32[]{:S(2)}) copy-start(f32[3072]{0:T(1024)} %get-tuple-element.93) | copy-start | bytes 36868
  943.9 80.2 %copy-start.24 = (f32[768]{0:T(1024)S(1)}, f32[768]{0:T(1024)}, u32[]{:S(2)}) copy-start(f32[768]{0:T(1024)} %convert_reduce_fusion) | copy-start | bytes 9220
  1040.0 720.9 %all-reduce.11.cloned.1.call-start = ((), (), s32[]{:S(2)}) async-start(), calls=%async_computation | async-start | bytes 14180352 | tf_op jit(solution)/shard_map/psum | solution.py:382
  1524.5 66.8 %slice-start.6 = ((s8[4841472]{0:T(1024)(128)(4,1)}), s8[647168]{0:T(1024)(128)(4,1)S(1)}, s32[]{:S(2)}) async-start(s8[4841472]{0:T(1024)(128)(4,1)} %bitcast.74), calls=%async_computation.9 | async-start | bytes 1294336
  1535.8 55.5 %slice-start.7 = ((s8[4841472]{0:T(1024)(128)(4,1)}), s8[4194304]{0:T(1024)(128)(4,1)S(1)}, s32[]{:S(2)}) async-start(s8[4841472]{0:T(1024)(128)(4,1)} %bitcast.74), calls=%async_computation.10 | async-start | bytes 8388608
  1535.8 55.5 %copy-start.27 = (f32[768]{0:T(1024)S(1)}, f32[768]{0:T(1024)}, u32[]{:S(2)}) copy-start(f32[768]{0:T(1024)} %get-tuple-element.64) | copy-start | bytes 9220
  1792.9 22.1 %copy-start.8 = (f32[1,590784]{1,0:T(1,128)S(1)}, f32[1,590784]{1,0:T(1,128)}, u32[]{:S(2)}) copy-start(f32[1,590784]{1,0:T(1,128)} %get-tuple-element.72) | copy-start | bytes 7089412
  1792.9 22.1 %copy-start.9 = (f32[1,590784]{1,0:T(1,128)S(1)}, f32[1,590784]{1,0:T(1,128)}, u32[]{:S(2)}) copy-start(f32[1,590784]{1,0:T(1,128)} %get-tuple-element.73) | copy-start | bytes 7089412
  1792.9 22.1 %copy-start.10 = (f32[590784]{0:T(1024)S(1)}, f32[590784]{0:T(1024)}, u32[]{:S(2)}) copy-start(f32[590784]{0:T(1024)} %get-tuple-element.104) | copy-start | bytes 7089412
  1792.9 22.1 %copy-start.11 = (f32[590784]{0:T(1024)S(1)}, f32[590784]{0:T(1024)}, u32[]{:S(2)}) copy-start(f32[590784]{0:T(1024)} %param.9) | copy-start | bytes 7089412
  1818.4 22.2 %slice-start.10 = ((s8[4726784]{0:T(1024)(128)(4,1)}), s8[4194304]{0:T(1024)(128)(4,1)S(1)}, s32[]{:S(2)}) async-start(s8[4726784]{0:T(1024)(128)(4,1)} %bitcast.78), calls=%async_computation.13 | async-start | bytes 8388608
  1825.7 14.9 slice-start.11
Sparse Core Ops, SparseCore 0:
  75.7 250.0 all-reduce.14
  1040.1 475.9 all-reduce.12
  1524.6 236.1 all-reduce.10
where the time goes:
time: 1880 us; the launch traced here: 1850 us
  waiting for transfers between devices  841 us (45%)
  local copies, waits for them, and re-layouts  571 us (30%)
  matrix products  253 us (13%)
  other arithmetic  167 us (9%)
    unnamed x5, waiting for transfers between devices  701 us
    unnamed x120, local copies, waits for them, and re-layouts  332 us
    psum x1, waiting for transfers between devices, body(): attn_total, feed_total = lax.psum((attn_share, feed_share), 'rep')  140 us
    dot_general x6, matrix products, product(): return jnp.einsum(form, left, right, preferred_element_type=jnp.float32)  109 us
    mul x1, other arithmetic, adam_change(): second_moment = beta_two * moments[1] + (1.0 - beta_two) * grads * grads  55.5 us
    dot_general x4, matrix products, times_transposed(): lax.dot_general(left, right, (((1,), (1,)), ((), ())), preferred_element_...  53 us
    dot_general x4, matrix products, transposed_times(): lax.dot_general(left, right, (((0,), (0,)), ((), ())), preferred_element_...  45.2 us
    another operation x2, local copies, waits for them, and re-layouts, adam_change(): return (change, jnp.stack([first_moment, second_moment]))  44.1 us
  transfers between devices with their start and end apart: 3, of which 3 were waited for; matrix products, arithmetic and copies ran while one was open for 6% of the time, Pallas kernels for 0%

commit v1 on v0

v1 whole, which is shorter than its diff:
```python
import functools

import jax
import jax.numpy as jnp
from jax import lax
from jax.experimental import pallas as pl
from jax.experimental.pallas import tpu as pltpu
from jax.sharding import PartitionSpec as P

D = 768
HEADS = 12
FF = 3072
T = 208

F32 = jnp.float32
BF = jnp.bfloat16

ln_eps = 1e-06
beta_one = 0.9
beta_two = 0.999
adam_eps = 1e-08
rate_matrix = 0.01
rate_vector = 0.1
decay_matrix = 0.05
root_half = 0.7071067811865476
inv_root_tau = 0.3989422804014327

MB = 1 << 20
LANES = 128
MARGIN = 8

ATTN_START = (12, 5, -3, 2)
FEED_START = (12, 2, 15, 5)


def attn_parts(share):
    if share < 3:
        return [(16, 256 * part, 6 * part, 18) for part in range(3)]
    return [(48, 0, 0, 6)]


def feed_parts(share):
    if share < 2:
        return [(24, 768 * j + 384 * h, 12 * h + 6 * j, 24) for j in range(2) for h in range(2)]
    return [(96, 0, 0, 6)]


ATTN_EXTRA = (
    [(0, 0, 12), (12, 4602, 14)],
    [(25, 0, 5), (30, 4613, 3)],
    [(33, 0, 15), (48, 4605, 11)],
    [(58, 0, 2), (60, 4610, 6)],
)
FEED_EXTRA = (
    [(0, 0, 12), (12, 9204, 23)],
    [(34, 0, 2), (36, 9218, 9)],
    [(45, 0, 15), (60, 9225, 2)],
    [(61, 0, 5), (66, 9221, 6)],
)
ATTN_PUT = (
    [(0, 0, 12)],
    [(25, 0, 5), (30, 4613, 3)],
    [(48, 4605, 12)],
    [(58, 0, 2), (60, 4610, 6)],
)
FEED_PUT = (
    [(0, 0, 12)],
    [(34, 0, 2), (36, 9218, 9)],
    [(45, 0, 15)],
    [(61, 0, 5), (66, 9221, 6)],
)
EXTRA = 72


class Block:
    def __init__(self, start, parts, extra, put, rows, matrices):
        self.start, self.parts, self.extra, self.put = start, parts, extra, put
        self.rows = rows
        self.matrices = matrices


ATTN = Block(ATTN_START, attn_parts, ATTN_EXTRA, ATTN_PUT, 768, ((1536, 1771008), (1772544, 2362368)))
FEED = Block(FEED_START, feed_parts, FEED_EXTRA, FEED_PUT, 1536, ((1536, 2360832), (2363904, 4723200)))


def params(limit=56):
    return pltpu.CompilerParams(vmem_limit_bytes=limit * MB)


def dot(a, b):
    return lax.dot_general(a, b, (((1,), (0,)), ((), ())), preferred_element_type=F32)


def dot_nt(a, b):
    return lax.dot_general(a, b, (((1,), (1,)), ((), ())), preferred_element_type=F32)


def dot_tn(a, b):
    return lax.dot_general(a, b, (((0,), (0,)), ((), ())), preferred_element_type=F32)


def normed_of(values):
    center = values - jnp.mean(values, axis=-1, keepdims=True)
    spread = lax.rsqrt(jnp.mean(center * center, axis=-1, keepdims=True) + ln_eps)
    return center * spread, spread


def whole(array):
    rank = len(array.shape)
    return pl.BlockSpec(array.shape, lambda *i: (0,) * rank, pipeline_mode=pl.Buffered(1))


def rows_of(count, width):
    return pl.BlockSpec((count, width), lambda i: (i, 0))


SMEM = pl.BlockSpec(memory_space=pltpu.SMEM)


def sds(shape, dtype):
    return jax.ShapeDtypeStruct(shape, dtype)


CHUNK = 512


def prep_kernel(block, steps, shard_ref, flat_ref, box_ref, extra_ref, held):
    step = pl.program_id(0)
    held[pl.ds(pl.multiple_of(MARGIN + CHUNK * step, 8), CHUNK), :] = flat_ref[...].reshape(CHUNK, LANES)

    @pl.when(step == steps - 1)
    def _():
        low = lax.broadcasted_iota(jnp.int32, (8, LANES), 1) < 64
        low_one = lax.broadcasted_iota(jnp.int32, (1, LANES), 1) < 64
        extra_ref[...] = jnp.zeros_like(extra_ref)
        for share in range(4):

            @pl.when(shard_ref[0] == share)
            def _(share=share):
                odd = share % 2 == 1

                def tile(first, stride):
                    here = held[pl.ds(first, 8, stride=stride), :]
                    if not odd:
                        return here
                    ahead = held[pl.ds(first - 1, 8, stride=stride), :]
                    return jnp.where(low, pltpu.roll(ahead, 64, 1), pltpu.roll(here, 64, 1))

                for groups, box_row, flat_row, stride in block.parts(share):
                    base = MARGIN + block.start[share] + flat_row

                    def body(group, carry, base=base, box_row=box_row, stride=stride):
                        for j in range(6):
                            first = base + 16 * stride * group + j
                            both = jnp.concatenate([tile(first, stride), tile(first + 8 * stride, stride)], axis=0)
                            at = pl.multiple_of(box_row + 16 * group, 16)
                            box_ref[pl.ds(at, 16), LANES * j : LANES * j + LANES] = both.astype(BF)
                        return carry

                    lax.fori_loop(0, groups, body, 0)
                count = flat_rows(block, share)
                for to, row, length in block.extra[share]:
                    for k in range(length):
                        at = MARGIN + row + k
                        value = held[at : at + 1, :]
                        if odd:
                            ahead = held[at - 1 : at, :]
                            value = jnp.where(low_one, pltpu.roll(ahead, 64, 1), pltpu.roll(value, 64, 1))
                            if row + k == 0:
                                value = jnp.where(low_one, 0.0, value)
                        elif row + k == count:
                            value = jnp.where(low_one, value, 0.0)
                        extra_ref[to + k : to + k + 1, :] = value.astype(BF).astype(F32)


def flat_rows(block, share):
    return 4615 if block is ATTN else 9226


def prep(block, flat, shard):
    steps = -(-flat.shape[0] // (CHUNK * LANES))
    return pl.pallas_call(
        functools.partial(prep_kernel, block, steps),
        grid=(steps,),
        in_specs=[SMEM, pl.BlockSpec((CHUNK * LANES,), lambda i: (i,))],
        out_specs=[
            pl.BlockSpec((block.rows, D), lambda i: (0, 0)),
            pl.BlockSpec((EXTRA, LANES), lambda i: (0, 0)),
        ],
        out_shape=[sds((block.rows, D), BF), sds((EXTRA, LANES), F32)],
        scratch_shapes=[pltpu.VMEM((MARGIN + CHUNK * steps + MARGIN, LANES), F32)],
        compiler_params=params(),
    )(shard, flat)


def spread_row(extra_ref, first, count):
    return jnp.concatenate([extra_ref[first + k : first + k + 1, :] for k in range(count)], axis=1)


def patch_row(ref, row, values):
    at = row // 16 * 16
    rows = lax.broadcasted_iota(jnp.int32, (16, values.shape[1]), 0)
    old = ref[at : at + 16, :].astype(F32)
    ref[at : at + 16, :] = jnp.where(rows == row - at, values, old).astype(BF)


def assemble_attn(shard_ref, extra_ref, a0, a1, a2, a3, qkv_ref, proj_ref, vec_ref, bias_ref, sems):
    shard = shard_ref[0]
    for wait in (False, True):
        for k, box in enumerate((a0, a1, a2, a3)):
            share = jnp.bitwise_xor(shard, k)

            @pl.when(share == 3)
            def _(box=box, k=k):
                copy = pltpu.make_async_copy(box, proj_ref, sems.at[k, 0])
                copy.wait() if wait else copy.start()

            @pl.when(share != 3)
            def _(box=box, k=k, share=share):
                for part in range(3):
                    copy = pltpu.make_async_copy(
                        box.at[pl.ds(256 * part, 256), :],
                        qkv_ref.at[pl.ds(pl.multiple_of(768 * part + 256 * share, 256), 256), :],
                        sems.at[k, part],
                    )
                    copy.wait() if wait else copy.start()

    for part in range(3):
        patch_row(qkv_ref, 768 * part + 255, spread_row(extra_ref, 12 + 6 * part, 6))
        patch_row(qkv_ref, 768 * part + 512, spread_row(extra_ref, 30 + 6 * part, 6))
    vec_ref[...] = jnp.zeros_like(vec_ref)
    for row, first in enumerate((0, 6, 60, EXTRA + 0, EXTRA + 6)):
        vec_ref[row : row + 1, :] = spread_row(extra_ref, first, 6)
    bias_ref[...] = jnp.zeros_like(bias_ref)
    bias_ref[0:1, 0:768] = spread_row(extra_ref, 48, 6)
    bias_ref[0:1, 1536:2304] = spread_row(extra_ref, 54, 6)


def call_assemble_attn(shard, extra, boxes):
    anywhere = pl.BlockSpec(memory_space=pl.ANY)
    return pl.pallas_call(
        assemble_attn,
        in_specs=[SMEM, pl.BlockSpec(memory_space=pltpu.VMEM)] + [anywhere] * 4,
        out_specs=[pl.BlockSpec(memory_space=pltpu.VMEM)] * 4,
        out_shape=[sds((2304, D), BF), sds((D, D), BF), sds((8, D), F32), sds((8, 2304), F32)],
        scratch_shapes=[pltpu.SemaphoreType.DMA((4, 3))],
        compiler_params=params(),
    )(shard, extra, *boxes)


def assemble_feed(shard_ref, extra_ref, a0, a1, a2, a3, up_ref, down_ref, ub_ref, db_ref, sems):
    shard = shard_ref[0]
    for wait in (False, True):
        for k, box in enumerate((a0, a1, a2, a3)):
            share = jnp.bitwise_xor(shard, k)

            @pl.when(share >= 2)
            def _(box=box, k=k, share=share):
                at = pl.multiple_of(1536 * (share - 2), 512)
                copy = pltpu.make_async_copy(box, down_ref.at[pl.ds(at, 1536), :], sems.at[k, 0])
                copy.wait() if wait else copy.start()

            @pl.when(share < 2)
            def _(box=box, k=k, share=share):
                for j in range(2):
                    for h in range(2):
                        copy = pltpu.make_async_copy(
                            box.at[pl.ds(768 * j + 384 * h, 384), :],
                            up_ref.at[pl.ds(pl.multiple_of(768 * (2 * h + j) + 384 * share, 128), 384), :],
                            sems.at[k, 2 * j + h],
                        )
                        copy.wait() if wait else copy.start()

    for part in range(4):
        patch_row(up_ref, 768 * part + 383, spread_row(extra_ref, EXTRA + 12 + 6 * part, 6))
    patch_row(down_ref, 1535, spread_row(extra_ref, EXTRA + 60, 6))
    ub_ref[...] = jnp.zeros_like(ub_ref)
    ub_ref[0:1, :] = spread_row(extra_ref, EXTRA + 36, 24)
    db_ref[...] = jnp.zeros_like(db_ref)
    db_ref[0:1, :] = spread_row(extra_ref, EXTRA + 66, 6)


def call_assemble_feed(shard, extra, boxes):
    anywhere = pl.BlockSpec(memory_space=pl.ANY)
    return pl.pallas_call(
        assemble_feed,
        in_specs=[SMEM, pl.BlockSpec(memory_space=pltpu.VMEM)] + [anywhere] * 4,
        out_specs=[pl.BlockSpec(memory_space=pltpu.VMEM)] * 4,
        out_shape=[sds((FF, D), BF), sds((FF, D), BF), sds((8, FF), F32), sds((8, D), F32)],
        scratch_shapes=[pltpu.SemaphoreType.DMA((4, 4))],
        compiler_params=params(),
    )(shard, extra, *boxes)


def attn_forward(seq, x_ref, vec_ref, bias_ref, qkv_w, proj_w, first_ref, qkv_ref, log_ref, att_ref, hid_ref, second_ref):
    x = x_ref[...].astype(F32)
    normed, _ = normed_of(x)
    first = (normed * vec_ref[0:1, :] + vec_ref[1:2, :]).astype(BF)
    first_ref[...] = first
    for part in range(3):
        cols = slice(768 * part, 768 * part + 768)
        qkv_ref[:, cols] = (dot(first, qkv_w[cols, :]) + bias_ref[0:1, cols]).astype(BF)
    low = lax.broadcasted_iota(jnp.int32, (T, LANES), 1) < 64
    real = lax.broadcasted_iota(jnp.int32, (T, T), 0) < seq
    for pair in range(HEADS // 2):
        at = LANES * pair
        q = qkv_ref[:, at : at + LANES] * jnp.asarray(0.125, BF)
        k = qkv_ref[:, 768 + at : 768 + at + LANES]
        v = qkv_ref[:, 1536 + at : 1536 + at + LANES]
        outs = []
        for half in range(2):
            own = low if half == 0 else ~low
            scores = dot_nt(k, jnp.where(own, q, jnp.zeros_like(q)))
            scores = jnp.where(real, scores, -1e30)
            top = jnp.max(scores, axis=0, keepdims=True)
            weight = jnp.exp(scores - top)
            total = jnp.sum(weight, axis=0, keepdims=True)
            head = 2 * pair + half
            log_ref[0, head : head + 1, :] = top + jnp.log(total)
            outs.append(dot_tn((weight * (1.0 / total)).astype(BF), v))
        att_ref[:, at : at + LANES] = jnp.where(low, outs[0], outs[1]).astype(BF)
    hidden = x + dot(att_ref[...], proj_w[...]) + vec_ref[2:3, :]
    hid_ref[...] = hidden
    normed, _ = normed_of(hidden)
    second_ref[...] = (normed * vec_ref[3:4, :] + vec_ref[4:5, :]).astype(BF)


def call_attn_forward(seq, x, vec, bias, qkv_w, proj_w):
    rows = x.shape[0]
    images = rows // T
    return pl.pallas_call(
        functools.partial(attn_forward, seq),
        grid=(images,),
        in_specs=[rows_of(T, D), whole(vec), whole(bias), whole(qkv_w), whole(proj_w)],
        out_specs=[
            rows_of(T, D),
            rows_of(T, 2304),
            pl.BlockSpec((1, HEADS, T), lambda i: (i, 0, 0)),
            rows_of(T, D),
            rows_of(T, D),
            rows_of(T, D),
        ],
        out_shape=[
            sds((rows, D), BF),
            sds((rows, 2304), BF),
            sds((images, HEADS, T), F32),
            sds((rows, D), BF),
            sds((rows, D), F32),
            sds((rows, D), BF),
        ],
        compiler_params=params(),
    )(x, vec, bias, qkv_w, proj_w)


def feed(seq, width, second_ref, cot_ref, hid_ref, up_w, ub_ref, down_w, db_ref, act_ref, pre_ref, out_ref, gs_ref, sum_ref, cot_sum):
    second = second_ref[...]
    cot = cot_ref[...]
    result = hid_ref[...] + db_ref[0:1, :]
    grad_second = jnp.zeros_like(result)

    @pl.when(pl.program_id(0) == 0)
    def _():
        sum_ref[...] = jnp.zeros_like(sum_ref)
        cot_sum[...] = jnp.zeros_like(cot_sum)

    cot_sum[0:1, :] += jnp.sum(cot.astype(F32), axis=0, keepdims=True)
    for part in range(FF // width):
        cols = slice(width * part, width * part + width)
        pre = dot(second, up_w[cols, :]) + ub_ref[0:1, cols]
        grad_act = dot_nt(cot, down_w[cols, :])
        half = 0.5 * (1.0 + lax.erf(pre * root_half))
        act = (pre * half).astype(BF)
        grad_pre = grad_act * (half + pre * jnp.exp(-0.5 * pre * pre) * inv_root_tau)
        low = grad_pre.astype(BF)
        act_ref[:, cols] = act
        pre_ref[:, cols] = low
        sum_ref[0:1, cols] += jnp.sum(grad_pre, axis=0, keepdims=True)
        result = result + dot(act, down_w[cols, :])
        grad_second = grad_second + dot_nt(low, up_w[cols, :])
    for image in range(result.shape[0] // T):
        out_ref[image] = result[T * image : T * image + seq].astype(BF)
    gs_ref[...] = grad_second


def call_feed(seq, second, cot, hidden, up_w, ub, down_w, db):
    rows = second.shape[0]
    images = rows // T
    step = 2 if images % 2 == 0 else 1
    tall = step * T
    return pl.pallas_call(
        functools.partial(feed, seq, D),
        grid=(images // step,),
        in_specs=[rows_of(tall, D)] * 3 + [whole(up_w), whole(ub), whole(down_w), whole(db)],
        out_specs=[
            rows_of(tall, FF),
            rows_of(tall, FF),
            pl.BlockSpec((step, seq, D), lambda i: (i, 0, 0)),
            rows_of(tall, D),
            pl.BlockSpec((8, FF), lambda i: (0, 0)),
            pl.BlockSpec((8, D), lambda i: (0, 0)),
        ],
        out_shape=[
            sds((rows, FF), BF),
            sds((rows, FF), BF),
            sds((images, seq, D), BF),
            sds((rows, D), F32),
            sds((8, FF), F32),
            sds((8, D), F32),
        ],
        compiler_params=params(),
    )(second, cot, hidden, up_w, ub, down_w, db)


def over_tokens(left_ref, right_ref, out_ref):
    out_ref[...] = dot_tn(left_ref[...], right_ref[...]).astype(out_ref.dtype).reshape(out_ref.shape)


def call_over_tokens(left, right, grid, left_block, right_block, out_shape, out_block):
    count = left.shape[0]
    return pl.pallas_call(
        over_tokens,
        grid=grid,
        in_specs=[
            pl.BlockSpec((count, left_block[0]), left_block[1]),
            pl.BlockSpec((count, right_block[0]), right_block[1]),
        ],
        out_specs=pl.BlockSpec(*out_block),
        out_shape=sds(out_shape, BF),
        compiler_params=params(),
    )(left, right)


def attn_backward(seq, gs_ref, hid_ref, cot_ref, log_ref, qkv_ref, vec_ref, proj_w, grad_ref, low_ref, gh_ref, sum_ref, head_sum, ga_ref):
    @pl.when(pl.program_id(0) == 0)
    def _():
        sum_ref[...] = jnp.zeros_like(sum_ref)
        head_sum[...] = jnp.zeros_like(head_sum)

    gs = gs_ref[...]
    normed, spread = normed_of(hid_ref[...])
    gn = gs * vec_ref[3:4, :]
    gh = cot_ref[...].astype(F32) + spread * (
        gn - jnp.mean(gn, axis=-1, keepdims=True) - normed * jnp.mean(gn * normed, axis=-1, keepdims=True)
    )
    sum_ref[0:1, :] += jnp.sum(gs * normed, axis=0, keepdims=True)
    sum_ref[1:2, :] += jnp.sum(gs, axis=0, keepdims=True)
    sum_ref[2:3, :] += jnp.sum(gh, axis=0, keepdims=True)
    gh_ref[...] = gh
    gh_low = gh.astype(BF)
    low_ref[...] = gh_low
    ga_ref[...] = dot_nt(gh_low, proj_w[...]).astype(BF)
    low = lax.broadcasted_iota(jnp.int32, (T, LANES), 1) < 64
    real = lax.broadcasted_iota(jnp.int32, (T, T), 0) < seq
    eighth = jnp.asarray(0.125, BF)
    for pair in range(HEADS // 2):
        at = LANES * pair
        cols = slice(at, at + LANES)
        q = qkv_ref[:, cols] * eighth
        k = qkv_ref[:, 768 + at : 768 + at + LANES]
        v = qkv_ref[:, 1536 + at : 1536 + at + LANES]
        k_small = k * eighth
        grad_out = ga_ref[:, cols]
        zero = jnp.zeros_like(q)
        grads = ([], [], [])
        for half in range(2):
            own = low if half == 0 else ~low
            head = 2 * pair + half
            scores = dot_nt(k, jnp.where(own, q, zero))
            probs = jnp.where(real, jnp.exp(scores - log_ref[0, head : head + 1, :]), 0.0)
            grads[2].append(dot(probs.astype(BF), grad_out))
            grad_probs = dot_nt(v, jnp.where(own, grad_out, zero))
            delta = jnp.sum(probs * grad_probs, axis=0, keepdims=True)
            grad_scores = (probs * (grad_probs - delta)).astype(BF)
            grads[1].append(dot(grad_scores, q))
            grads[0].append(dot_tn(grad_scores, k_small))
        for part in range(3):
            grad = jnp.where(low, grads[part][0], grads[part][1])
            if part != 1:
                row = part // 2
                head_sum[row : row + 1, cols] += jnp.sum(grad, axis=0, keepdims=True)
            grad_ref[:, 768 * part + at : 768 * part + at + LANES] = grad.astype(BF)


def call_attn_backward(seq, gs, hidden, cot, log_total, qkv, vec, proj_w):
    rows = gs.shape[0]
    small = pl.BlockSpec((8, D), lambda i: (0, 0))
    return pl.pallas_call(
        functools.partial(attn_backward, seq),
        grid=(rows // T,),
        in_specs=[rows_of(T, D)] * 3
        + [pl.BlockSpec((1, HEADS, T), lambda i: (i, 0, 0)), rows_of(T, 2304), whole(vec), whole(proj_w)],
        out_specs=[rows_of(T, 2304), rows_of(T, D), rows_of(T, D), small, small],
        out_shape=[sds((rows, 2304), BF), sds((rows, D), BF), sds((rows, D), F32), sds((8, D), F32), sds((8, D), F32)],
        scratch_shapes=[pltpu.VMEM((T, D), BF)],
        compiler_params=params(),
    )(gs, hidden, cot, log_total, qkv, vec, proj_w)


def input_backward(seq, grad_ref, gh_ref, x_ref, vec_ref, qkv_w, out_ref, sum_ref):
    @pl.when(pl.program_id(0) == 0)
    def _():
        sum_ref[...] = jnp.zeros_like(sum_ref)

    grad_first = dot_nt(grad_ref[:, 0:768], qkv_w[0:768, :])
    for part in range(1, 3):
        cols = slice(768 * part, 768 * part + 768)
        grad_first = grad_first + dot_nt(grad_ref[:, cols], qkv_w[cols, :])
    normed, spread = normed_of(x_ref[...].astype(F32))
    gn = grad_first * vec_ref[0:1, :]
    grad = gh_ref[...] + spread * (
        gn - jnp.mean(gn, axis=-1, keepdims=True) - normed * jnp.mean(gn * normed, axis=-1, keepdims=True)
    )
    sum_ref[0:1, :] += jnp.sum(grad_first * normed, axis=0, keepdims=True)
    sum_ref[1:2, :] += jnp.sum(grad_first, axis=0, keepdims=True)
    for image in range(grad.shape[0] // T):
        out_ref[image] = grad[T * image : T * image + seq].astype(BF)


def call_input_backward(seq, grad, gh, x, vec, qkv_w):
    rows = gh.shape[0]
    images = rows // T
    step = 2 if images % 2 == 0 else 1
    tall = step * T
    return pl.pallas_call(
        functools.partial(input_backward, seq),
        grid=(images // step,),
        in_specs=[rows_of(tall, 2304), rows_of(tall, D), rows_of(tall, D), whole(vec), whole(qkv_w)],
        out_specs=[pl.BlockSpec((step, seq, D), lambda i: (i, 0, 0)), pl.BlockSpec((8, D), lambda i: (0, 0))],
        out_shape=[sds((images, seq, D), BF), sds((8, D), F32)],
        compiler_params=params(),
    )(grad, gh, x, vec, qkv_w)


def put_row(out_ref, first, values):
    for k in range(values.shape[1] // LANES):
        out_ref[first + k : first + k + 1, :] = values[:, LANES * k : LANES * k + LANES]


def pack_attn(last_sum, back_sum, head_sum, qkv_grad, out_ref):
    out_ref[...] = jnp.zeros_like(out_ref)
    put_row(out_ref, 0, last_sum[0:1, :])
    put_row(out_ref, 6, last_sum[1:2, :])
    for part in range(3):
        at = 256 * part
        put_row(out_ref, 12 + 6 * part, qkv_grad[0, at + 240 : at + 256, :].astype(F32)[15:16])
        put_row(out_ref, 30 + 6 * part, qkv_grad[2, at : at + 16, :].astype(F32)[0:1])
    put_row(out_ref, 48, head_sum[0:1, :])
    put_row(out_ref, 54, head_sum[1:2, :])
    put_row(out_ref, 60, back_sum[2:3, :])


def pack_feed(back_sum, pre_sum, cot_sum, up0, up1, down1, out_ref):
    put_row(out_ref, 0, back_sum[0:1, :])
    put_row(out_ref, 6, back_sum[1:2, :])
    for j, up in enumerate((up0, up1)):
        for h in range(2):
            put_row(out_ref, 12 + 12 * h + 6 * j, up[0, 384 * h + 368 : 384 * h + 384, :].astype(F32)[15:16])
    put_row(out_ref, 36, pre_sum[0:1, :])
    put_row(out_ref, 60, down1[0, 752:768, :].astype(F32)[15:16])
    put_row(out_ref, 66, cot_sum[0:1, :])


def call_pack(kernel, *arrays):
    return pl.pallas_call(
        kernel,
        in_specs=[pl.BlockSpec(memory_space=pltpu.VMEM)] * len(arrays),
        out_specs=pl.BlockSpec(memory_space=pltpu.VMEM),
        out_shape=sds((EXTRA, LANES), F32),
        compiler_params=params(),
    )(*arrays)


def adam_kernel(block, share_size, scale, boxes, shard_ref, power_ref, extra_ref, *refs):
    box_refs = refs[:boxes]
    flat_ref, mom_ref, grad_ref, change_ref, new_ref, held = refs[boxes:]
    step = pl.program_id(0)

    @pl.when(step == 0)
    def _():
        for share in range(4):

            @pl.when(shard_ref[0] == share)
            def _(share=share):
                for groups, box_row, flat_row, stride in block.parts(share):
                    base = MARGIN + block.start[share] + flat_row
                    for index in range(boxes):
                        first = max(box_row, 768 * index)
                        end = min(box_row + 16 * groups, 768 * index + 768)
                        if first >= end:
                            continue

                        def body(group, carry, index=index, first=first, base=base, box_row=box_row, stride=stride):
                            row = pl.multiple_of(first - 768 * index + 16 * group, 16)
                            for j in range(6):
                                both = box_refs[index][pl.ds(row, 16), LANES * j : LANES * j + LANES].astype(F32)
                                at = base + stride * (first - box_row + 16 * group) + j
                                held[pl.ds(at, 8, stride=stride), :] = both[0:8]
                                held[pl.ds(at + 8 * stride, 8, stride=stride), :] = both[8:16]
                            return carry

                        lax.fori_loop(0, (end - first) // 16, body, 0)
                for source, row, length in block.put[share]:
                    held[MARGIN + row : MARGIN + row + length, :] = extra_ref[source : source + length, :]

    start = pl.multiple_of(MARGIN + CHUNK * step, 8)
    shard = shard_ref[0]
    low = lax.broadcasted_iota(jnp.int32, (CHUNK, LANES), 1) < 64
    here = held[pl.ds(start, CHUNK), :]
    after = held[pl.ds(start + 1, CHUNK), :]
    shifted = jnp.where(low, pltpu.roll(here, 64, 1), pltpu.roll(after, 64, 1))
    grad = jnp.where(shard % 2 == 1, shifted, here) * scale
    position = (
        shard * share_size
        + step * (CHUNK * LANES)
        + lax.broadcasted_iota(jnp.int32, (CHUNK, LANES), 0) * LANES
        + lax.broadcasted_iota(jnp.int32, (CHUNK, LANES), 1)
    )
    matrix = jnp.zeros((CHUNK, LANES), jnp.bool_)
    for first, end in block.matrices:
        matrix = matrix | ((position >= first) & (position < end))
    size = CHUNK * LANES
    p = flat_ref[...].reshape(CHUNK, LANES)
    m = beta_one * mom_ref[0, :].reshape(CHUNK, LANES) + (1.0 - beta_one) * grad
    s = beta_two * mom_ref[1, :].reshape(CHUNK, LANES) + (1.0 - beta_two) * grad * grad
    ratio = (m * power_ref[0]) / (jnp.sqrt(s * power_ref[1]) + adam_eps)
    change = jnp.where(matrix, rate_matrix, rate_vector) * (ratio + jnp.where(matrix, decay_matrix, 0.0) * p)
    grad_ref[...] = grad.reshape(size)
    change_ref[...] = change.reshape(size)
    new_ref[0, :] = m.reshape(size)
    new_ref[1, :] = s.reshape(size)


def adam(block, shard, powers, extra, boxes, flat, moments, scale):
    count = flat.shape[0]
    steps = -(-count // (CHUNK * LANES))
    line = pl.BlockSpec((CHUNK * LANES,), lambda i: (i,))
    two = pl.BlockSpec((2, CHUNK * LANES), lambda i: (0, i))
    return pl.pallas_call(
        functools.partial(adam_kernel, block, count, scale, len(boxes)),
        grid=(steps,),
        in_specs=[SMEM, SMEM, whole(extra)] + [whole(box) for box in boxes] + [line, two],
        out_specs=[line, line, two],
        out_shape=[sds((count,), F32), sds((count,), F32), sds((2, count), F32)],
        scratch_shapes=[pltpu.VMEM((MARGIN + CHUNK * steps + MARGIN, LANES), F32)],
        compiler_params=params(),
    )(shard, powers, extra, *boxes, flat, moments)


def swap(value, axis, bit):
    pairs = [(i, i ^ bit) for i in range(lax.axis_size(axis))]
    return lax.ppermute(value, axis, pairs)


def turn(value, axis, unit, distance):
    size = lax.axis_size(axis)
    return lax.ppermute(value, axis, [(i, (i + unit * distance) % size) for i in range(size)])


def pick(array, index, axis=0):
    return lax.dynamic_index_in_dim(array, index, axis, keepdims=False)


def reduce_share(pieces):
    shard = lax.axis_index("shard")
    core, side = shard % 2, shard // 2
    rep = lax.axis_index("rep")
    near, far = rep % 2, rep // 2
    count = lax.axis_size("rep") // 2
    rows = pieces[0].shape[0]
    on = core == 0
    other = jnp.stack([jnp.where(on, pieces[1], pieces[0]), jnp.where(on, pieces[3], pieces[2])])
    mine = jnp.stack([jnp.where(on, pieces[0], pieces[1]), jnp.where(on, pieces[2], pieces[3])])
    came = swap(other, "shard", 1)
    total = mine.astype(F32) + came.astype(F32)
    came = swap(pick(total, 1 - side).astype(BF), "shard", 2)
    total = pick(total, side) + came.astype(F32)
    halves = total.reshape(2, rows // 2, D)
    came = swap(pick(halves, 1 - near).astype(BF), "rep", 1)
    half = pick(halves, near) + came.astype(F32)
    parts = half.reshape(count, rows // 2 // count, D)
    arrived = [
        turn(pick(parts, (far + step) % count).astype(BF), "rep", 2, step) for step in range(1, count)
    ]
    part = pick(parts, far)
    for value in arrived:
        part = part + value.astype(F32)
    part = part.astype(BF)
    others = [turn(part, "rep", 2, step) for step in range(1, count)]
    full = jnp.zeros((count, rows // 2 // count, D), BF)
    for step, value in enumerate([part] + others):
        full = lax.dynamic_update_slice_in_dim(full, value[None], (far + count - step) % count, 0)
    half = full.reshape(rows // 2, D)
    came = swap(half, "rep", 1)
    first = near == 0
    return jnp.concatenate([jnp.where(first, half, came), jnp.where(first, came, half)], axis=0)


def reduce_all(value):
    value = value + swap(value, "shard", 1)
    value = value + swap(value, "shard", 2)
    bit = 1
    while bit < lax.axis_size("rep"):
        value = value + swap(value, "rep", bit)
        bit *= 2
    return value


def gather_boxes(box):
    across = swap(box, "shard", 2)
    return box, swap(box, "shard", 1), across, swap(across, "shard", 1)


def body(layer_input, out_cotangent, attention_params, attention_moments, feedforward_params, feedforward_moments, step_count):
    images, seq, _ = layer_input.shape
    image_total = images * lax.axis_size("shard") * lax.axis_size("rep")
    scale = 1.0 / image_total
    shard = lax.axis_index("shard").astype(jnp.int32).reshape(1)
    attn_box, attn_extra = prep(ATTN, attention_params, shard)
    feed_box, feed_extra = prep(FEED, feedforward_params, shard)
    extra = jnp.concatenate([attn_extra, feed_extra], axis=0)
    extra = extra + swap(extra, "shard", 1)
    extra = extra + swap(extra, "shard", 2)
    pad = ((0, 0), (0, T - seq), (0, 0))
    x = jnp.pad(layer_input, pad).reshape(images * T, D)
    cot = jnp.pad(out_cotangent, pad).reshape(images * T, D)
    qkv_w, proj_w, vec, bias = call_assemble_attn(shard, extra, gather_boxes(attn_box))
    first, qkv, log_total, attended, hidden, second = call_attn_forward(seq, x, vec, bias, qkv_w, proj_w)
    up_w, down_w, ub, db = call_assemble_feed(shard, extra, gather_boxes(feed_box))
    act, pre, layer_output, gs, pre_sum, cot_sum = call_feed(seq, second, cot, hidden, up_w, ub, down_w, db)
    feed_boxes, ups, downs = [], [], []
    for j in range(2):
        up = call_over_tokens(
            second, pre, (2, 2), (384, lambda s, h: (0, s)), (768, lambda s, h, j=j: (0, 2 * h + j)),
            (2, 768, D), ((1, 384, D), lambda s, h: (s, h, 0)),
        )
        down = call_over_tokens(
            act, cot, (2,), (768, lambda s, j=j: (0, 2 * s + j)), (768, lambda s: (0, 0)),
            (2, 768, D), ((1, 768, D), lambda s: (s, 0, 0)),
        )
        ups.append(up)
        downs.append(down)
        feed_boxes.append(reduce_share([up[0], up[1], down[0], down[1]]))
    qkv_grad, gh_low, gh, back_sum, head_sum = call_attn_backward(seq, gs, hidden, cot, log_total, qkv, vec, proj_w)
    proj_grad = call_over_tokens(
        attended, gh_low, (1,), (768, lambda i: (0, 0)), (768, lambda i: (0, 0)), (D, D), ((D, D), lambda i: (0, 0)),
    )
    weight_grad = call_over_tokens(
        first, qkv_grad, (3, 3), (256, lambda s, b: (0, s)), (768, lambda s, b: (0, b)),
        (3, 768, D), ((1, 256, D), lambda s, b: (s, b, 0)),
    )
    attn_total = reduce_share([weight_grad[0], weight_grad[1], weight_grad[2], proj_grad])
    input_grad, last_sum = call_input_backward(seq, qkv_grad, gh, x, vec, qkv_w)
    feed_sums = reduce_all(call_pack(pack_feed, back_sum, pre_sum, cot_sum, ups[0], ups[1], downs[1]))
    attn_sums = reduce_all(call_pack(pack_attn, last_sum, back_sum, head_sum, weight_grad))
    time = step_count[0].astype(F32)
    powers = jnp.stack([1.0 / (1.0 - jnp.power(beta_one, time)), 1.0 / (1.0 - jnp.power(beta_two, time))])
    feed_grad, feed_change, feed_new = adam(
        FEED, shard, powers, feed_sums, feed_boxes, feedforward_params, feedforward_moments, scale
    )
    attn_grad, attn_change, attn_new = adam(
        ATTN, shard, powers, attn_sums, [attn_total], attention_params, attention_moments, scale
    )
    return (layer_output, input_grad, attn_grad, feed_grad, attn_change, attn_new, feed_change, feed_new)


def solution(mesh):
    tokens = P(("shard", "rep"), None, None)
    in_specs = (tokens, tokens, P("shard"), P(None, "shard"), P("shard"), P(None, "shard"), P())
    out_specs = (tokens, tokens, P("shard"), P("shard"), P("shard"), P(None, "shard"), P("shard"), P(None, "shard"))
    return jax.shard_map(body, mesh=mesh, in_specs=in_specs, out_specs=out_specs, check_vma=False)
```

time: 1880 us -> 584 us (0.31); the launches traced: 1850 us -> 578 us
  waiting for transfers between devices: 841 us -> 169 us
  local copies, waits for them, and re-layouts: 571 us -> 24.6 us
  Pallas kernels: 0 us -> 255 us
  matrix products: 253 us -> 0 us
  other arithmetic: 167 us -> 31.2 us
  starting transfers between devices: 0.12 us -> 95.2 us
    unnamed x5 -> x0, waiting for transfers between devices: 701 us -> none
    unnamed x120 -> x43, local copies, waits for them, and re-layouts: 332 us -> 14.5 us
    pallas_call x0 -> x18, Pallas kernels: none -> 255 us  [the longest x6 57 us: call_over_tokens(): pl.pallas_call(over_tokens, grid=grid, in_specs=[pl.BlockSpec((count, lef...]
    dot_general x18 -> x0, matrix products: 253 us -> none  [the longest x6 109 us: product(): return jnp.einsum(form, left, right, preferred_element_type=jnp.float32)]
    ppermute x0 -> x48, waiting for transfers between devices: none -> 169 us  [the longest x30 144 us: swap(): return lax.ppermute(value, axis, pairs)]
    psum x1 -> x0, waiting for transfers between devices: 140 us -> none  [body(): attn_total, feed_total = lax.psum((attn_share, feed_share), 'rep')]
    reshape x17 -> x0, local copies, waits for them, and re-layouts: 114 us -> none  [the longest x2 17.2 us: forward_pass(): key_part = projected[:, model_width:2 * model_width].reshape(head_shape)]
    ppermute x0 -> x48, starting transfers between devices: none -> 95.2 us  [the longest x30 56.7 us: swap(): return lax.ppermute(value, axis, pairs)]
  transfers between devices with their start and end apart: 3 -> 48, of which waited for: 3 -> 16; matrix products, arithmetic and copies ran while one was open for 6% -> 8% of each run, Pallas kernels for 0% -> 21%
where the time goes in v1:
time: 584 us; the launch traced here: 578 us
  Pallas kernels  255 us (44%)
  waiting for transfers between devices  169 us (29%)
  starting transfers between devices  95.2 us (16%)
  other arithmetic  31.2 us (5%)
  local copies, waits for them, and re-layouts  24.6 us (4%)
    ppermute x30, waiting for transfers between devices, swap(): return lax.ppermute(value, axis, pairs)  144 us
    pallas_call x6, Pallas kernels, call_over_tokens(): pl.pallas_call(over_tokens, grid=grid, in_specs=[pl.BlockSpec((count, lef...  57 us
    ppermute x30, starting transfers between devices, swap(): return lax.ppermute(value, axis, pairs)  56.7 us
    pallas_call x1, Pallas kernels, call_feed(): pl.pallas_call(functools.partial(feed, seq, D), grid=(images // step,), i...  42 us
    pallas_call x1, Pallas kernels, call_attn_backward(): pl.pallas_call(functools.partial(attn_backward, seq), grid=(rows // T,),...  40.2 us
    ppermute x18, starting transfers between devices, turn(): lax.ppermute(value, axis, [(i, (i + unit * distance) % size) for i in ran...  38.5 us
    pallas_call x2, Pallas kernels, adam(): pl.pallas_call(functools.partial(adam_kernel, block, count, scale, len(bo...  35.7 us
    pallas_call x1, Pallas kernels, call_attn_forward(): pl.pallas_call(functools.partial(attn_forward, seq), grid=(images,), in_s...  27.4 us
  transfers between devices with their start and end apart: 48, of which 16 were waited for; matrix products, arithmetic and copies ran while one was open for 8% of the time, Pallas kernels for 21%

profile of v1, /device:TPU:0, one launch (start us, length us, event | category | flops | bytes accessed | tf_op | source)
XLA Modules:
  0.0 577.6 jit_solution(15332138043217845680)
XLA Ops:
  0.6 12.4 %shard_map.135 = (bf16[1536,768]{1,0:T(8,128)(2,1)}, f32[72,128]{1,0:T(8,128)}) custom-call(s32[1]{0:T(128)} %bitcast.1.shard_ref, f32[1180992]{0:T(1024)} %refs_2_.3), custom_call_target="tpu_custom_call" | custom-call | tf_op jit(solution)/shard_map/pallas_call | solution.py:182
  13.0 2.5 collective-permute-start.6
  15.6 6.4 %shard_map.134 = (bf16[768,768]{1,0:T(8,128)(2,1)}, f32[72,128]{1,0:T(8,128)}) custom-call(s32[1]{0:T(128)} %bitcast.1.shard_ref, f32[590784]{0:T(1024)} %refs_1_.1), custom_call_target="tpu_custom_call" | custom-call | tf_op jit(solution)/shard_map/pallas_call | solution.py:182
  22.1 10.5 %collective-permute-start.5 = (bf16[1536,768]{1,0:T(8,128)(2,1)}, bf16[1536,768]{1,0:T(8,128)(2,1)}, u32[]{:S(2)}, u32[]{:S(2)}) collective-permute-start(bf16[1536,768]{1,0:T(8,128)(2,1)} %get-tuple-element.54.a0), channel_id=1, source_target_pairs={{0,8},{8,0},{16,24},{24,16},{1,9},{9,1},{17,25},{25,17},{2,10},{10... | collective-permute-start | bytes 7077896 | tf_op jit(solution)/shard_map/ppermute | solution.py:651
  32.6 28.9 %collective-permute-done.6.a2 = bf16[1536,768]{1,0:T(8,128)(2,1)} collective-permute-done((bf16[1536,768]{1,0:T(8,128)(2,1)}, bf16[1536,768]{1,0:T(8,128)(2,1)}, u32[]{:S(2)}, u32[]{:S(2)}) %collective-permute-start.6) | collective-permute-done | bytes 2359328 | tf_op jit(solution)/shard_map/ppermute | solution.py:651
  61.5 13.0 %collective-permute-start.7 = (bf16[1536,768]{1,0:T(8,128)(2,1)}, bf16[1536,768]{1,0:T(8,128)(2,1)}, u32[]{:S(2)}, u32[]{:S(2)}) collective-permute-start(bf16[1536,768]{1,0:T(8,128)(2,1)} %collective-permute-done.6.a2), channel_id=1, source_target_pairs={{0,8},{8,0},{16,24},{24,16},{1,9},{9,1},{17,25},{25,17},{2,10},{10... | collective-permute-start | bytes 7077896 | tf_op jit(solution)/shard_map/ppermute | solution.py:651
  74.5 12.3 %collective-permute-done.3.a2 = bf16[768,768]{1,0:T(8,128)(2,1)} collective-permute-done((bf16[768,768]{1,0:T(8,128)(2,1)}, bf16[768,768]{1,0:T(8,128)(2,1)}, u32[]{:S(2)}, u32[]{:S(2)}) %collective-permute-start.3) | collective-permute-done | bytes 1179680 | tf_op jit(solution)/shard_map/ppermute | solution.py:651
  86.8 6.3 %collective-permute-start.4 = (bf16[768,768]{1,0:T(8,128)(2,1)}, bf16[768,768]{1,0:T(8,128)(2,1)}, u32[]{:S(2)}, u32[]{:S(2)}) collective-permute-start(bf16[768,768]{1,0:T(8,128)(2,1)} %collective-permute-done.3.a2), channel_id=1, source_target_pairs={{0,8},{8,0},{16,24},{24,16},{1,9},{9,1},{17,25},{25,17},{2,10},{10... | collective-permute-start | bytes 3538952 | tf_op jit(solution)/shard_map/ppermute | solution.py:651
  95.9 2.1 collective-permute-start.1
  98.0 1.9 copy.19
  100.8 3.4 pad.7.clone
  104.2 1.6 pad.8.clone
  106.4 5.5 shard_map.136
  112.0 27.4 %shard_map.137 = (bf16[1664,768]{1,0:T(8,128)(2,1)}, bf16[1664,2304]{1,0:T(8,128)(2,1)}, f32[8,12,208]{2,1,0:T(8,128)}, bf16[1664,768]{1,0:T(8,128)(2,1)}, f32[1...) custom-call(bf16[1664,768]{1,0:T(8,128)(2,1)} %bitcast.125, f32[8,768]{1,0:T(8,128)} %get-tuple-element.48.vec_ref, ...), custom_call_target="tpu_custom_call" | custom-call | tf_op jit(solution)/shard_map/pallas_call | solution.py:331
  139.4 8.6 %shard_map.138 = (bf16[3072,768]{1,0:T(8,128)(2,1)}, bf16[3072,768]{1,0:T(8,128)(2,1)}, f32[8,3072]{1,0:T(8,128)}, f32[8,768]{1,0:T(8,128)}) custom-call(s32[1]{0:T(128)} %bitcast.1.shard_ref, f32[144,128]{1,0:T(8,128)} %add.232.extra_ref, bf16[1536,768]{1,0:T(8,128)(2,1)} %get-tuple-element.54.a0, bf16[1536,768]{1,0:T(8,128)(2,1)} %collective-permute-done.5.a1, ...), custom_call_target="tpu_custom_call" | custom-call | tf_op jit(solution)/shard_map/pallas_call | solution.py:285
  148.0 42.0 %shard_map.139 = (bf16[1664,3072]{1,0:T(8,128)(2,1)}, bf16[1664,3072]{1,0:T(8,128)(2,1)}, bf16[8,197,768]{2,1,0:T(8,128)(2,1)}, f32[1664,768]{1,0:T(8,128)}, f32[8,3072]{1,0:T(8,128)}, /*index=5*/f32[8,768]{1,0:T(8,128)}) custom-call(bf16[1664,768]{1,0:T(8,128)(2,1)} %get-tuple-element.52.second_ref.left_ref, bf16[1664,768]{1,0:T(8,128)(2,1)} %bitcast.121, ...), custom_call_target="tpu_custom_call" | custom-call | tf_op jit(solution)/shard_map/pallas_call | solution.py:390
  190.0 9.4 %shard_map.147.up1 = bf16[2,768,768]{2,1,0:T(8,128)(2,1)} custom-call(bf16[1664,768]{1,0:T(8,128)(2,1)} %get-tuple-element.52.second_ref.left_ref, bf16[1664,3072]{1,0:T(8,128)(2,1)} %get-tuple-element.75.right_ref), custom_call_target="tpu_custom_call" | custom-call | tf_op jit(solution)/shard_map/pallas_call | solution.py:420
  199.4 9.3 %shard_map.146.up0 = bf16[2,768,768]{2,1,0:T(8,128)(2,1)} custom-call(bf16[1664,768]{1,0:T(8,128)(2,1)} %get-tuple-element.52.second_ref.left_ref, bf16[1664,3072]{1,0:T(8,128)(2,1)} %get-tuple-element.75.right_ref), custom_call_target="tpu_custom_call" | custom-call | tf_op jit(solution)/shard_map/pallas_call | solution.py:420
  208.6 8.2 %shard_map.148.down1 = bf16[2,768,768]{2,1,0:T(8,128)(2,1)} custom-call(bf16[1664,3072]{1,0:T(8,128)(2,1)} %get-tuple-element.76.left_ref, bf16[1664,768]{1,0:T(8,128)(2,1)} %bitcast.122), custom_call_target="tpu_custom_call" | custom-call | tf_op jit(solution)/shard_map/pallas_call | solution.py:420
  216.9 8.6 %shard_map.150 = bf16[2,768,768]{2,1,0:T(8,128)(2,1)} custom-call(bf16[1664,3072]{1,0:T(8,128)(2,1)} %get-tuple-element.76.left_ref, bf16[1664,768]{1,0:T(8,128)(2,1)} %bitcast.123), custom_call_target="tpu_custom_call" | custom-call | tf_op jit(solution)/shard_map/pallas_call | solution.py:420
  228.3 1.6 pad_maximum_fusion.2
  231.9 1.6 pad_maximum_fusion.1
  233.5 40.2 %shard_map.140 = (bf16[1664,2304]{1,0:T(8,128)(2,1)}, bf16[1664,768]{1,0:T(8,128)(2,1)}, f32[1664,768]{1,0:T(8,128)}, f32[8,768]{1,0:T(8,128)}, f32[8,768]{1,0:T(8,128)}) custom-call(f32[1664,768]{1,0:T(8,128)} %get-tuple-element.60.gs_ref, f32[1664,768]{1,0:T(8,128)} %get-tuple-element.53.hid_ref, bf16[1664,768]{1,0:T(8,128)(2,1)} %bitcast.124, ...), custom_call_target="tpu_custom_call" | custom-call | tf_op jit(solution)/shard_map/pallas_call | solution.py:487
  273.8 15.7 %shard_map.142.qkv_grad = bf16[3,768,768]{2,1,0:T(8,128)(2,1)} custom-call(bf16[1664,768]{1,0:T(8,128)(2,1)} %get-tuple-element.69.left_ref, bf16[1664,2304]{1,0:T(8,128)(2,1)} %get-tuple-element.63.grad_ref.right_ref), custom_call_target="tpu_custom_call" | custom-call | tf_op jit(solution)/shard_map/pallas_call | solution.py:420
  289.5 2.8 broadcast_select_fusion.9
  292.3 5.8 %shard_map.144 = bf16[768,768]{1,0:T(8,128)(2,1)} custom-call(bf16[1664,768]{1,0:T(8,128)(2,1)} %get-tuple-element.70.left_ref, bf16[1664,768]{1,0:T(8,128)(2,1)} %get-tuple-element.71.right_ref), custom_call_target="tpu_custom_call" | custom-call | tf_op jit(solution)/shard_map/pallas_call | solution.py:420
  298.1 2.8 select_bitcast_fusion.1
  303.1 2.4 convert_add_fusion
  306.8 2.8 convert_add_fusion.1
  313.0 2.2 convert_add_fusion.2
  319.1 3.8 shard_map.149
  322.9 13.1 %shard_map.141 = (bf16[8,197,768]{2,1,0:T(8,128)(2,1)}, f32[8,768]{1,0:T(8,128)}) custom-call(bf16[1664,2304]{1,0:T(8,128)(2,1)} %get-tuple-element.63.grad_ref.right_ref, f32[1664,768]{1,0:T(8,128)} %get-tuple-element.64.gh_ref, bf16[1664,768]{1,0:T(8,128)(2,1)} %bitcast.126, f32[8,768]{1,0:T(8,128)} %get-tuple-element.48.vec_ref, ...), custom_call_target="tpu_custom_call" | custom-call | tf_op jit(solution)/shard_map/pallas_call | solution.py:524
  336.0 2.7 shard_map.143
  342.1 44.6 %collective-permute-done.24 = f32[72,128]{1,0:T(8,128)S(1)} collective-permute-done((f32[72,128]{1,0:T(8,128)S(1)}, f32[72,128]{1,0:T(8,128)S(1)}, u32[]{:S(2)}, u32[]{:S(2)}) %collective-permute-start.24) | collective-permute-done | bytes 36896 | tf_op jit(solution)/shard_map/ppermute | solution.py:651
  388.7 1.9 collective-permute-done.25
  392.2 1.6 collective-permute-start.11
  394.7 2.6 collective-permute-start.27
  397.3 1.7 collective-permute-start.12
  399.6 3.7 copy.18
  403.4 1.9 copy.17
  409.6 1.6 bitcast_add_fusion.1
  412.0 1.6 bitcast_add_fusion.2
  415.2 9.3 %collective-permute-done.40 = bf16[384,768]{1,0:T(8,128)(2,1)S(1)} collective-permute-done((bf16[384,768]{1,0:T(8,128)(2,1)S(1)}, bf16[384,768]{1,0:T(8,128)(2,1)S(1)}, u32[]{:S(2)}, u32[]{:S(2)}) %collective-permute-start.40) | collective-permute-done | bytes 589856 | tf_op jit(solution)/shard_map/ppermute | solution.py:651
  428.9 8.2 %collective-permute-done.30 = bf16[384,768]{1,0:T(8,128)(2,1)S(1)} collective-permute-done((bf16[384,768]{1,0:T(8,128)(2,1)S(1)}, bf16[384,768]{1,0:T(8,128)(2,1)S(1)}, u32[]{:S(2)}, u32[]{:S(2)}) %collective-permute-start.30) | collective-permute-done | bytes 589856 | tf_op jit(solution)/shard_map/ppermute | solution.py:651
  438.8 5.7 collective-permute-done.15
  444.5 2.1 collective-permute-start.32
  446.8 1.9 collective-permute-start.33
  449.9 2.8 collective-permute-start.18
  452.7 8.6 %collective-permute-done.32 = bf16[96,768]{1,0:T(8,128)(2,1)S(1)} collective-permute-done((bf16[96,768]{1,0:T(8,128)(2,1)S(1)}, bf16[96,768]{1,0:T(8,128)(2,1)S(1)}, u32[]{:S(2)}, u32[]{:S(2)}) %collective-permute-start.32) | collective-permute-done | bytes 147488 | tf_op jit(solution)/shard_map/ppermute | solution.py:656
  461.3 3.3 collective-permute-start.45
  464.7 3.4 collective-permute-start.46
  468.2 4.8 collective-permute-done.17
  473.9 5.0 collective-permute-start.35
  479.1 1.7 collective-permute-start.36
  480.8 4.8 collective-permute-done.45
  486.8 5.2 collective-permute-start.20
  492.0 2.5 collective-permute-done.19
  494.6 4.1 collective-permute-start.21
  498.6 4.3 collective-permute-done.20
  504.2 2.1 collective-permute-start.22
  506.5 25.3 %collective-permute-done.22 = bf16[384,768]{1,0:T(8,128)(2,1)S(1)} collective-permute-done((bf16[384,768]{1,0:T(8,128)(2,1)S(1)}, bf16[384,768]{1,0:T(8,128)(2,1)S(1)}, u32[]{:S(2)}, u32[]{:S(2)}) %collective-permute-start.22) | collective-permute-done | bytes 589856 | tf_op jit(solution)/shard_map/ppermute | solution.py:651
  533.1 6.6 %collective-permute-done.37 = bf16[384,768]{1,0:T(8,128)(2,1)S(1)} collective-permute-done((bf16[384,768]{1,0:T(8,128)(2,1)S(1)}, bf16[384,768]{1,0:T(8,128)(2,1)S(1)}, u32[]{:S(2)}, u32[]{:S(2)}) %collective-permute-start.37) | collective-permute-done | bytes 589856 | tf_op jit(solution)/shard_map/ppermute | solution.py:651
  541.4 12.2 %shard_map.145 = (f32[590784]{0:T(1024)}, f32[590784]{0:T(1024)}, f32[2,590784]{1,0:T(2,128)}) custom-call(s32[1]{0:T(128)} %bitcast.1.shard_ref, f32[2]{0:T(128)} %pad_maximum_fusion.6.power_ref, f32[72,128]{1,0:T(8,128)} %add.237.extra_ref, bf16[768,768]{1,0:T(8,128)(2,1)} %pad_maximum_fusion.3.refs_0_, f32[590784]{0:T(1024)} %refs_1_.1, f32[2,590784]{1,0:T(2,128)} %refs_2_.2), custom_call_target="tpu_custom_call" | custom-call | tf_op jit(solution)/shard_map/pallas_call | solution.py:638
  553.6 23.5 %shard_map.151 = (f32[1180992]{0:T(1024)}, f32[1180992]{0:T(1024)}, f32[2,1180992]{1,0:T(2,128)}) custom-call(s32[1]{0:T(128)} %bitcast.1.shard_ref, f32[2]{0:T(128)} %pad_maximum_fusion.6.power_ref, f32[72,128]{1,0:T(8,128)} %add.266.extra_ref, bf16[768,768]{1,0:T(8,128)(2,1)} %get-tuple-element.123.refs_0_, bf16[768,768]{1,0:T(8,128)(2,1)} %get-tuple-element.124.refs_1_, ...), custom_call_target="tpu_custom_call" | custom-call | tf_op jit(solution)/shard_map/pallas_call | solution.py:638
  (159 shorter events, 48.7 us)
Async XLA Ops:
  13.0 84.9 %copy-start.10 = (bf16[8,197,768]{2,0,1:T(8,128)(2,1)S(1)}, bf16[8,197,768]{2,0,1:T(8,128)(2,1)}, u32[]{:S(2)}) copy-start(bf16[8,197,768]{2,0,1:T(8,128)(2,1)} %param.7) | copy-start | bytes 7262212
  13.0 48.5 %collective-permute-start.6 = (bf16[1536,768]{1,0:T(8,128)(2,1)}, bf16[1536,768]{1,0:T(8,128)(2,1)}, u32[]{:S(2)}, u32[]{:S(2)}) collective-permute-start(bf16[1536,768]{1,0:T(8,128)(2,1)} %get-tuple-element.54.a0), channel_id=1, source_target_pairs={{0,16},{8,24},{16,0},{24,8},{1,17},{9,25},{17,1},{25,9},{2,18},{10... | collective-permute-start | bytes 7077896 | tf_op jit(solution)/shard_map/ppermute | solution.py:651
  22.0 64.8 %collective-permute-start.3 = (bf16[768,768]{1,0:T(8,128)(2,1)}, bf16[768,768]{1,0:T(8,128)(2,1)}, u32[]{:S(2)}, u32[]{:S(2)}) collective-permute-start(bf16[768,768]{1,0:T(8,128)(2,1)} %get-tuple-element.47.a0), channel_id=1, source_target_pairs={{0,16},{8,24},{16,0},{24,8},{1,17},{9,25},{17,1},{25,9},{2,18},{10... | collective-permute-start | bytes 3538952 | tf_op jit(solution)/shard_map/ppermute | solution.py:651
  22.1 117.3 %collective-permute-start.5 = (bf16[1536,768]{1,0:T(8,128)(2,1)}, bf16[1536,768]{1,0:T(8,128)(2,1)}, u32[]{:S(2)}, u32[]{:S(2)}) collective-permute-start(bf16[1536,768]{1,0:T(8,128)(2,1)} %get-tuple-element.54.a0), channel_id=1, source_target_pairs={{0,8},{8,0},{16,24},{24,16},{1,9},{9,1},{17,25},{25,17},{2,10},{10... | collective-permute-start | bytes 7077896 | tf_op jit(solution)/shard_map/ppermute | solution.py:651
  61.5 77.9 %collective-permute-start.7 = (bf16[1536,768]{1,0:T(8,128)(2,1)}, bf16[1536,768]{1,0:T(8,128)(2,1)}, u32[]{:S(2)}, u32[]{:S(2)}) collective-permute-start(bf16[1536,768]{1,0:T(8,128)(2,1)} %collective-permute-done.6.a2), channel_id=1, source_target_pairs={{0,8},{8,0},{16,24},{24,16},{1,9},{9,1},{17,25},{25,17},{2,10},{10... | collective-permute-start | bytes 7077896 | tf_op jit(solution)/shard_map/ppermute | solution.py:651
  74.5 31.9 %collective-permute-start.2 = (bf16[768,768]{1,0:T(8,128)(2,1)}, bf16[768,768]{1,0:T(8,128)(2,1)}, u32[]{:S(2)}, u32[]{:S(2)}) collective-permute-start(bf16[768,768]{1,0:T(8,128)(2,1)} %get-tuple-element.47.a0), channel_id=1, source_target_pairs={{0,8},{8,0},{16,24},{24,16},{1,9},{9,1},{17,25},{25,17},{2,10},{10... | collective-permute-start | bytes 3538952 | tf_op jit(solution)/shard_map/ppermute | solution.py:651
  86.8 19.6 %collective-permute-start.4 = (bf16[768,768]{1,0:T(8,128)(2,1)}, bf16[768,768]{1,0:T(8,128)(2,1)}, u32[]{:S(2)}, u32[]{:S(2)}) collective-permute-start(bf16[768,768]{1,0:T(8,128)(2,1)} %collective-permute-done.3.a2), channel_id=1, source_target_pairs={{0,8},{8,0},{16,24},{24,16},{1,9},{9,1},{17,25},{25,17},{2,10},{10... | collective-permute-start | bytes 3538952 | tf_op jit(solution)/shard_map/ppermute | solution.py:651
  94.6 1.3 collective-permute-start
  95.9 9.9 %collective-permute-start.1 = (f32[144,128]{1,0:T(8,128)S(1)}, f32[144,128]{1,0:T(8,128)S(1)}, u32[]{:S(2)}, u32[]{:S(2)}) collective-permute-start(f32[144,128]{1,0:T(8,128)S(1)} %add.231), channel_id=1, source_target_pairs={{0,16},{8,24},{16,0},{24,8},{1,17},{9,25},{17,1},{25,9},{2,18},{10... | collective-permute-start | bytes 221192 | tf_op jit(solution)/shard_map/ppermute | solution.py:651
  216.9 8.6 %copy-start = (bf16[2,768,768]{2,1,0:T(8,128)(2,1)S(1)}, bf16[2,768,768]{2,1,0:T(8,128)(2,1)}, u32[]{:S(2)}) copy-start(bf16[2,768,768]{2,1,0:T(8,128)(2,1)} %shard_map.147.up1) | copy-start | bytes 7077892
  228.3 2.5 copy-start.1
  229.9 73.1 %collective-permute-start.38 = (bf16[2,768,768]{2,1,0:T(8,128)(2,1)}, bf16[2,768,768]{2,1,0:T(8,128)(2,1)}, u32[]{:S(2)}, u32[]{:S(2)}) collective-permute-start(bf16[2,768,768]{2,1,0:T(8,128)(2,1)} %pad_maximum_fusion.2), channel_id=1, source_target_pairs={{0,8},{8,0},{16,24},{24,16},{1,9},{9,1},{17,25},{25,17},{2,10},{10... | collective-permute-start | bytes 7077896 | tf_op jit(solution)/shard_map/ppermute | solution.py:651
  233.5 73.3 %collective-permute-start.28 = (bf16[2,768,768]{2,1,0:T(8,128)(2,1)}, bf16[2,768,768]{2,1,0:T(8,128)(2,1)}, u32[]{:S(2)}, u32[]{:S(2)}) collective-permute-start(bf16[2,768,768]{2,1,0:T(8,128)(2,1)} %pad_maximum_fusion.1), channel_id=1, source_target_pairs={{0,8},{8,0},{16,24},{24,16},{1,9},{9,1},{17,25},{25,17},{2,10},{10... | collective-permute-start | bytes 7077896 | tf_op jit(solution)/shard_map/ppermute | solution.py:651
  302.5 9.7 %collective-permute-start.13 = (bf16[2,768,768]{2,1,0:T(8,128)(2,1)}, bf16[2,768,768]{2,1,0:T(8,128)(2,1)}, u32[]{:S(2)}, u32[]{:S(2)}) collective-permute-start(bf16[2,768,768]{2,1,0:T(8,128)(2,1)} %pad_maximum_fusion), channel_id=1, source_target_pairs={{0,8},{8,0},{16,24},{24,16},{1,9},{9,1},{17,25},{25,17},{2,10},{10... | collective-permute-start | bytes 7077896 | tf_op jit(solution)/shard_map/ppermute | solution.py:651
  305.5 4.1 copy-start.3
  306.8 99.7 %collective-permute-start.39 = (bf16[768,768]{1,0:T(8,128)(2,1)}, bf16[768,768]{1,0:T(8,128)(2,1)}, u32[]{:S(2)}, u32[]{:S(2)}) collective-permute-start(bf16[768,768]{1,0:T(8,128)(2,1)} %fusion.2), channel_id=1, source_target_pairs={{0,16},{8,24},{16,0},{24,8},{1,17},{9,25},{17,1},{25,9},{2,18},{10... | collective-permute-start | bytes 3538952 | tf_op jit(solution)/shard_map/ppermute | solution.py:651
  309.6 5.5 copy-start.4
  309.6 2.6 copy-start.7
  309.6 3.3 copy-start.8
  310.9 98.7 %collective-permute-start.29 = (bf16[768,768]{1,0:T(8,128)(2,1)}, bf16[768,768]{1,0:T(8,128)(2,1)}, u32[]{:S(2)}, u32[]{:S(2)}) collective-permute-start(bf16[768,768]{1,0:T(8,128)(2,1)} %fusion.1), channel_id=1, source_target_pairs={{0,16},{8,24},{16,0},{24,8},{1,17},{9,25},{17,1},{25,9},{2,18},{10... | collective-permute-start | bytes 3538952 | tf_op jit(solution)/shard_map/ppermute | solution.py:651
  315.2 2.5 copy-start.5
  317.7 94.3 %collective-permute-start.14 = (bf16[768,768]{1,0:T(8,128)(2,1)}, bf16[768,768]{1,0:T(8,128)(2,1)}, u32[]{:S(2)}, u32[]{:S(2)}) collective-permute-start(bf16[768,768]{1,0:T(8,128)(2,1)} %fusion), channel_id=1, source_target_pairs={{0,16},{8,24},{16,0},{24,8},{1,17},{9,25},{17,1},{25,9},{2,18},{10... | collective-permute-start | bytes 3538952 | tf_op jit(solution)/shard_map/ppermute | solution.py:651
  322.9 16.3 %collective-permute-start.23 = (f32[72,128]{1,0:T(8,128)}, f32[72,128]{1,0:T(8,128)S(1)}, u32[]{:S(2)}, u32[]{:S(2)}) collective-permute-start(f32[72,128]{1,0:T(8,128)} %shard_map.149), channel_id=1, source_target_pairs={{0,8},{8,0},{16,24},{24,16},{1,9},{9,1},{17,25},{25,17},{2,10},{10... | collective-permute-start | bytes 110600 | tf_op jit(solution)/shard_map/ppermute | solution.py:651
  336.0 3.2 copy-start.12
  338.7 1.6 collective-permute-start.8
  339.2 47.4 %collective-permute-start.24 = (f32[72,128]{1,0:T(8,128)S(1)}, f32[72,128]{1,0:T(8,128)S(1)}, u32[]{:S(2)}, u32[]{:S(2)}) collective-permute-start(f32[72,128]{1,0:T(8,128)S(1)} %add.262), channel_id=1, source_target_pairs={{0,16},{8,24},{16,0},{24,8},{1,17},{9,25},{17,1},{25,9},{2,18},{10... | collective-permute-start | bytes 110600 | tf_op jit(solution)/shard_map/ppermute | solution.py:651
  341.0 47.1 %collective-permute-start.9 = (f32[72,128]{1,0:T(8,128)S(1)}, f32[72,128]{1,0:T(8,128)S(1)}, u32[]{:S(2)}, u32[]{:S(2)}) collective-permute-start(f32[72,128]{1,0:T(8,128)S(1)} %add.233), channel_id=1, source_target_pairs={{0,16},{8,24},{16,0},{24,8},{1,17},{9,25},{17,1},{25,9},{2,18},{10... | collective-permute-start | bytes 110600 | tf_op jit(solution)/shard_map/ppermute | solution.py:651
  386.6 4.0 collective-permute-start.25
  388.1 15.2 %copy-start.9 = (bf16[8,197,768]{2,1,0:T(8,128)(2,1)S(1)}, bf16[8,197,768]{2,1,0:T(8,128)(2,1)}, u32[]{:S(2)}) copy-start(bf16[8,197,768]{2,1,0:T(8,128)(2,1)} %get-tuple-element.82) | copy-start | bytes 7262212
  388.1 4.0 collective-permute-start.10
  390.6 4.0 collective-permute-start.26
  392.2 14.3 %slice-start = ((s8[4718592]{0:T(1024)(128)(4,1)}), s8[524288]{0:T(1024)(128)(4,1)S(1)}, s32[]{:S(2)}) async-start(s8[4718592]{0:T(1024)(128)(4,1)} %bitcast.127), calls=%async_computation | async-start | bytes 1048576
  392.2 5.1 collective-permute-start.11
  394.7 10.6 %collective-permute-start.27 = (f32[72,128]{1,0:T(8,128)S(1)}, f32[72,128]{1,0:T(8,128)S(1)}, u32[]{:S(2)}, u32[]{:S(2)}) collective-permute-start(f32[72,128]{1,0:T(8,128)S(1)} %add.265), channel_id=1, source_target_pairs={{0,4},{1,5},{2,6},{3,7},{4,0},{5,1},{6,2},{7,3},{8,12},{9,13},{10,... | collective-permute-start | bytes 110600 | tf_op jit(solution)/shard_map/ppermute | solution.py:651
  397.3 8.6 %collective-permute-start.12 = (f32[72,128]{1,0:T(8,128)S(1)}, f32[72,128]{1,0:T(8,128)S(1)}, u32[]{:S(2)}, u32[]{:S(2)}) collective-permute-start(f32[72,128]{1,0:T(8,128)S(1)} %add.236), channel_id=1, source_target_pairs={{0,4},{1,5},{2,6},{3,7},{4,0},{5,1},{6,2},{7,3},{8,12},{9,13},{10,... | collective-permute-start | bytes 110600 | tf_op jit(solution)/shard_map/ppermute | solution.py:651
  399.6 6.9 %slice-start.1 = ((s8[4718592]{0:T(1024)(128)(4,1)}), s8[4194304]{0:T(1024)(128)(4,1)S(1)}, s32[]{:S(2)}) async-start(s8[4718592]{0:T(1024)(128)(4,1)} %bitcast.127), calls=%async_computation.1 | async-start | bytes 8388608
  399.6 10.0 %slice-start.2 = ((s8[4718592]{0:T(1024)(128)(4,1)}), s8[4194304]{0:T(1024)(128)(4,1)S(1)}, s32[]{:S(2)}) async-start(s8[4718592]{0:T(1024)(128)(4,1)} %bitcast.129), calls=%async_computation.2 | async-start | bytes 8388608
  403.4 6.2 %slice-start.3 = ((s8[4718592]{0:T(1024)(128)(4,1)}), s8[524288]{0:T(1024)(128)(4,1)S(1)}, s32[]{:S(2)}) async-start(s8[4718592]{0:T(1024)(128)(4,1)} %bitcast.129), calls=%async_computation.3 | async-start | bytes 1048576
  403.4 8.7 %slice-start.4 = ((s8[4718592]{0:T(1024)(128)(4,1)}), s8[4194304]{0:T(1024)(128)(4,1)S(1)}, s32[]{:S(2)}) async-start(s8[4718592]{0:T(1024)(128)(4,1)} %bitcast.131), calls=%async_computation.4 | async-start | bytes 8388608
  406.5 5.5 slice-start.5
  408.2 16.3 %collective-permute-start.40 = (bf16[384,768]{1,0:T(8,128)(2,1)S(1)}, bf16[384,768]{1,0:T(8,128)(2,1)S(1)}, u32[]{:S(2)}, u32[]{:S(2)}) collective-permute-start(bf16[384,768]{1,0:T(8,128)(2,1)S(1)} %fusion.5), channel_id=1, source_target_pairs={{0,1},{1,0},{2,3},{3,2},{4,5},{5,4},{6,7},{7,6},{8,9},{9,8},{10,11... | collective-permute-start | bytes 1769480 | tf_op jit(solution)/shard_map/ppermute | solution.py:651
  411.3 25.8 %collective-permute-start.30 = (bf16[384,768]{1,0:T(8,128)(2,1)S(1)}, bf16[384,768]{1,0:T(8,128)(2,1)S(1)}, u32[]{:S(2)}, u32[]{:S(2)}) collective-permute-start(bf16[384,768]{1,0:T(8,128)(2,1)S(1)} %fusion.4), channel_id=1, source_target_pairs={{0,1},{1,0},{2,3},{3,2},{4,5},{5,4},{6,7},{7,6},{8,9},{9,8},{10,11... | collective-permute-start | bytes 1769480 | tf_op jit(solution)/shard_map/ppermute | solution.py:651
  413.7 30.8 %collective-permute-start.15 = (bf16[384,768]{1,0:T(8,128)(2,1)S(1)}, bf16[384,768]{1,0:T(8,128)(2,1)S(1)}, u32[]{:S(2)}, u32[]{:S(2)}) collective-permute-start(bf16[384,768]{1,0:T(8,128)(2,1)S(1)} %fusion.3), channel_id=1, source_target_pairs={{0,1},{1,0},{2,3},{3,2},{4,5},{5,4},{6,7},{7,6},{8,9},{9,8},{10,11... | collective-permute-start | bytes 1769480 | tf_op jit(solution)/shard_map/ppermute | solution.py:651
  424.7 22.2 %collective-permute-start.41 = (bf16[96,768]{1,0:T(8,128)(2,1)S(1)}, bf16[96,768]{1,0:T(8,128)(2,1)S(1)}, u32[]{:S(2)}, u32[]{:S(2)}) collective-permute-start(bf16[96,768]{1,0:T(8,128)(2,1)S(1)} %get-tuple-element.110), channel_id=1, source_target_pairs={{0,2},{1,3},{2,4},{3,5},{4,6},{5,7},{6,0},{7,1},{8,10},{9,11},{10,... | collective-permute-start | bytes 442376 | tf_op jit(solution)/shard_map/ppermute | solution.py:656
  426.2 22.5 %collective-permute-start.42 = (bf16[96,768]{1,0:T(8,128)(2,1)S(1)}, bf16[96,768]{1,0:T(8,128)(2,1)S(1)}, u32[]{:S(2)}, u32[]{:S(2)}) collective-permute-start(bf16[96,768]{1,0:T(8,128)(2,1)S(1)} %get-tuple-element.112), channel_id=1, source_target_pairs={{0,4},{1,5},{2,6},{3,7},{4,0},{5,1},{6,2},{7,3},{8,12},{9,13},{10,... | collective-permute-start | bytes 442376 | tf_op jit(solution)/shard_map/ppermute | solution.py:656
  427.4 21.5 %collective-permute-start.43 = (bf16[96,768]{1,0:T(8,128)(2,1)S(1)}, bf16[96,768]{1,0:T(8,128)(2,1)S(1)}, u32[]{:S(2)}, u32[]{:S(2)}) collective-permute-start(bf16[96,768]{1,0:T(8,128)(2,1)S(1)} %get-tuple-element.111), channel_id=1, source_target_pairs={{0,6},{1,7},{2,0},{3,1},{4,2},{5,3},{6,4},{7,5},{8,14},{9,15},{10,... | collective-permute-start | bytes 442376 | tf_op jit(solution)/shard_map/ppermute | solution.py:656
  437.3 12.6 %collective-permute-start.31 = (bf16[96,768]{1,0:T(8,128)(2,1)S(1)}, bf16[96,768]{1,0:T(8,128)(2,1)S(1)}, u32[]{:S(2)}, u32[]{:S(2)}) collective-permute-start(bf16[96,768]{1,0:T(8,128)(2,1)S(1)} %get-tuple-element.115), channel_id=1, source_target_pairs={{0,2},{1,3},{2,4},{3,5},{4,6},{5,7},{6,0},{7,1},{8,10},{9,11},{10,... | collective-permute-start | bytes 442376 | tf_op jit(solution)/shard_map/ppermute | solution.py:656
  444.5 16.8 %collective-permute-start.32 = (bf16[96,768]{1,0:T(8,128)(2,1)S(1)}, bf16[96,768]{1,0:T(8,128)(2,1)S(1)}, u32[]{:S(2)}, u32[]{:S(2)}) collective-permute-start(bf16[96,768]{1,0:T(8,128)(2,1)S(1)} %get-tuple-element.117), channel_id=1, source_target_pairs={{0,4},{1,5},{2,6},{3,7},{4,0},{5,1},{6,2},{7,3},{8,12},{9,13},{10,... | collective-permute-start | bytes 442376 | tf_op jit(solution)/shard_map/ppermute | solution.py:656
  446.8 14.5 %collective-permute-start.33 = (bf16[96,768]{1,0:T(8,128)(2,1)S(1)}, bf16[96,768]{1,0:T(8,128)(2,1)S(1)}, u32[]{:S(2)}, u32[]{:S(2)}) collective-permute-start(bf16[96,768]{1,0:T(8,128)(2,1)S(1)} %get-tuple-element.116), channel_id=1, source_target_pairs={{0,6},{1,7},{2,0},{3,1},{4,2},{5,3},{6,4},{7,5},{8,14},{9,15},{10,... | collective-permute-start | bytes 442376 | tf_op jit(solution)/shard_map/ppermute | solution.py:656
  448.7 16.0 %collective-permute-start.16 = (bf16[96,768]{1,0:T(8,128)(2,1)S(1)}, bf16[96,768]{1,0:T(8,128)(2,1)S(1)}, u32[]{:S(2)}, u32[]{:S(2)}) collective-permute-start(bf16[96,768]{1,0:T(8,128)(2,1)S(1)} %get-tuple-element.120), channel_id=1, source_target_pairs={{0,2},{1,3},{2,4},{3,5},{4,6},{5,7},{6,0},{7,1},{8,10},{9,11},{10,... | collective-permute-start | bytes 442376 | tf_op jit(solution)/shard_map/ppermute | solution.py:656
  448.9 24.0 %collective-permute-start.17 = (bf16[96,768]{1,0:T(8,128)(2,1)S(1)}, bf16[96,768]{1,0:T(8,128)(2,1)S(1)}, u32[]{:S(2)}, u32[]{:S(2)}) collective-permute-start(bf16[96,768]{1,0:T(8,128)(2,1)S(1)} %get-tuple-element.122), channel_id=1, source_target_pairs={{0,4},{1,5},{2,6},{3,7},{4,0},{5,1},{6,2},{7,3},{8,12},{9,13},{10,... | collective-permute-start | bytes 442376 | tf_op jit(solution)/shard_map/ppermute | solution.py:656
  449.9 24.0 %collective-permute-start.18 = (bf16[96,768]{1,0:T(8,128)(2,1)S(1)}, bf16[96,768]{1,0:T(8,128)(2,1)S(1)}, u32[]{:S(2)}, u32[]{:S(2)}) collective-permute-start(bf16[96,768]{1,0:T(8,128)(2,1)S(1)} %get-tuple-element.121), channel_id=1, source_target_pairs={{0,6},{1,7},{2,0},{3,1},{4,2},{5,3},{6,4},{7,5},{8,14},{9,15},{10,... | collective-permute-start | bytes 442376 | tf_op jit(solution)/shard_map/ppermute | solution.py:656
  461.3 17.7 %collective-permute-start.44 = (bf16[96,768]{1,0:T(8,128)(2,1)S(1)}, bf16[96,768]{1,0:T(8,128)(2,1)S(1)}, u32[]{:S(2)}, u32[]{:S(2)}) collective-permute-start(bf16[96,768]{1,0:T(8,128)(2,1)S(1)} %get-tuple-element.91), channel_id=1, source_target_pairs={{0,2},{1,3},{2,4},{3,5},{4,6},{5,7},{6,0},{7,1},{8,10},{9,11},{10,... | collective-permute-start | bytes 442376 | tf_op jit(solution)/shard_map/ppermute | solution.py:656
  461.3 24.3 %collective-permute-start.45 = (bf16[96,768]{1,0:T(8,128)(2,1)S(1)}, bf16[96,768]{1,0:T(8,128)(2,1)S(1)}, u32[]{:S(2)}, u32[]{:S(2)}) collective-permute-start(bf16[96,768]{1,0:T(8,128)(2,1)S(1)} %get-tuple-element.91), channel_id=1, source_target_pairs={{0,4},{1,5},{2,6},{3,7},{4,0},{5,1},{6,2},{7,3},{8,12},{9,13},{10,... | collective-permute-start | bytes 442376 | tf_op jit(solution)/shard_map/ppermute | solution.py:656
  464.7 22.1 %collective-permute-start.46 = (bf16[96,768]{1,0:T(8,128)(2,1)S(1)}, bf16[96,768]{1,0:T(8,128)(2,1)S(1)}, u32[]{:S(2)}, u32[]{:S(2)}) collective-permute-start(bf16[96,768]{1,0:T(8,128)(2,1)S(1)} %get-tuple-element.91), channel_id=1, source_target_pairs={{0,6},{1,7},{2,0},{3,1},{4,2},{5,3},{6,4},{7,5},{8,14},{9,15},{10,... | collective-permute-start | bytes 442376 | tf_op jit(solution)/shard_map/ppermute | solution.py:656
  472.9 33.3 %collective-permute-start.34 = (bf16[96,768]{1,0:T(8,128)(2,1)S(1)}, bf16[96,768]{1,0:T(8,128)(2,1)S(1)}, u32[]{:S(2)}, u32[]{:S(2)}) collective-permute-start(bf16[96,768]{1,0:T(8,128)(2,1)S(1)} %get-tuple-element.93), channel_id=1, source_target_pairs={{0,2},{1,3},{2,4},{3,5},{4,6},{5,7},{6,0},{7,1},{8,10},{9,11},{10,... | collective-permute-start | bytes 442376 | tf_op jit(solution)/shard_map/ppermute | solution.py:656
  473.9 32.4 %collective-permute-start.35 = (bf16[96,768]{1,0:T(8,128)(2,1)S(1)}, bf16[96,768]{1,0:T(8,128)(2,1)S(1)}, u32[]{:S(2)}, u32[]{:S(2)}) collective-permute-start(bf16[96,768]{1,0:T(8,128)(2,1)S(1)} %get-tuple-element.93), channel_id=1, source_target_pairs={{0,4},{1,5},{2,6},{3,7},{4,0},{5,1},{6,2},{7,3},{8,12},{9,13},{10,... | collective-permute-start | bytes 442376 | tf_op jit(solution)/shard_map/ppermute | solution.py:656
  479.1 27.3 %collective-permute-start.36 = (bf16[96,768]{1,0:T(8,128)(2,1)S(1)}, bf16[96,768]{1,0:T(8,128)(2,1)S(1)}, u32[]{:S(2)}, u32[]{:S(2)}) collective-permute-start(bf16[96,768]{1,0:T(8,128)(2,1)S(1)} %get-tuple-element.93), channel_id=1, source_target_pairs={{0,6},{1,7},{2,0},{3,1},{4,2},{5,3},{6,4},{7,5},{8,14},{9,15},{10,... | collective-permute-start | bytes 442376 | tf_op jit(solution)/shard_map/ppermute | solution.py:656
  485.6 9.0 %collective-permute-start.19 = (bf16[96,768]{1,0:T(8,128)(2,1)S(1)}, bf16[96,768]{1,0:T(8,128)(2,1)S(1)}, u32[]{:S(2)}, u32[]{:S(2)}) collective-permute-start(bf16[96,768]{1,0:T(8,128)(2,1)S(1)} %get-tuple-element.95), channel_id=1, source_target_pairs={{0,2},{1,3},{2,4},{3,5},{4,6},{5,7},{6,0},{7,1},{8,10},{9,11},{10,... | collective-permute-start | bytes 442376 | tf_op jit(solution)/shard_map/ppermute | solution.py:656
  486.8 16.1 %collective-permute-start.20 = (bf16[96,768]{1,0:T(8,128)(2,1)S(1)}, bf16[96,768]{1,0:T(8,128)(2,1)S(1)}, u32[]{:S(2)}, u32[]{:S(2)}) collective-permute-start(bf16[96,768]{1,0:T(8,128)(2,1)S(1)} %get-tuple-element.95), channel_id=1, source_target_pairs={{0,4},{1,5},{2,6},{3,7},{4,0},{5,1},{6,2},{7,3},{8,12},{9,13},{10,... | collective-permute-start | bytes 442376 | tf_op jit(solution)/shard_map/ppermute | solution.py:656
  494.6 9.6 %collective-permute-start.21 = (bf16[96,768]{1,0:T(8,128)(2,1)S(1)}, bf16[96,768]{1,0:T(8,128)(2,1)S(1)}, u32[]{:S(2)}, u32[]{:S(2)}) collective-permute-start(bf16[96,768]{1,0:T(8,128)(2,1)S(1)} %get-tuple-element.95), channel_id=1, source_target_pairs={{0,6},{1,7},{2,0},{3,1},{4,2},{5,3},{6,4},{7,5},{8,14},{9,15},{10,... | collective-permute-start | bytes 442376 | tf_op jit(solution)/shard_map/ppermute | solution.py:656
  502.9 30.1 %collective-permute-start.47 = (bf16[384,768]{1,0:T(8,128)(2,1)S(1)}, bf16[384,768]{1,0:T(8,128)(2,1)S(1)}, u32[]{:S(2)}, u32[]{:S(2)}) collective-permute-start(bf16[384,768]{1,0:T(8,128)(2,1)S(1)} %bitcast.146), channel_id=1, source_target_pairs={{0,1},{1,0},{2,3},{3,2},{4,5},{5,4},{6,7},{7,6},{8,9},{9,8},{10,11... | collective-permute-start | bytes 1769480 | tf_op jit(solution)/shard_map/ppermute | solution.py:651
  504.2 27.6 %collective-permute-start.22 = (bf16[384,768]{1,0:T(8,128)(2,1)S(1)}, bf16[384,768]{1,0:T(8,128)(2,1)S(1)}, u32[]{:S(2)}, u32[]{:S(2)}) collective-permute-start(bf16[384,768]{1,0:T(8,128)(2,1)S(1)} %bitcast.145), channel_id=1, source_target_pairs={{0,1},{1,0},{2,3},{3,2},{4,5},{5,4},{6,7},{7,6},{8,9},{9,8},{10,11... | collective-permute-start | bytes 1769480 | tf_op jit(solution)/shard_map/ppermute | solution.py:651
  506.4 33.4 %collective-permute-start.37 = (bf16[384,768]{1,0:T(8,128)(2,1)S(1)}, bf16[384,768]{1,0:T(8,128)(2,1)S(1)}, u32[]{:S(2)}, u32[]{:S(2)}) collective-permute-start(bf16[384,768]{1,0:T(8,128)(2,1)S(1)} %bitcast.147), channel_id=1, source_target_pairs={{0,1},{1,0},{2,3},{3,2},{4,5},{5,4},{6,7},{7,6},{8,9},{9,8},{10,11... | collective-permute-start | bytes 1769480 | tf_op jit(solution)/shard_map/ppermute | solution.py:651
  (3 other events, 5.8 us)
